TPU v7x, 128 devices: a whole 4x4x4 slice. The times are simulated.
128 devices in a mesh: gx: 4 (over x_hi, core), gy: 32 (over y, z, x_lo).
Axes of the slice: x: 4 (x_hi: 2, x_lo: 2; x = x_hi * 2 + x_lo), y: 4, z: 4, core: 2. Of those that a mesh axis runs over, the one named last changes fastest.
Arguments:
- normed: bfloat16 [512, 14848], P(None, 'gx'), may hold values from -6 to 6
- residual: bfloat16 [512, 14848], P('gy', 'gx'), may hold values from -6 to 6
- w_query: bfloat16 [14848, 4, 32, 64], P('gx', None, 'gy'), may hold values from -0.046875 to 0.046875
- w_keyval: bfloat16 [14848, 4, 256], P('gx', None, 'gy'), may hold values from -0.046875 to 0.046875
- w_out: bfloat16 [32, 4, 64, 14848], P('gy', None, None, 'gx'), may hold values from -0.0625 to 0.0625
- w_up: bfloat16 [14848, 32768], P('gx', 'gy'), may hold values from -0.046875 to 0.046875
- w_down: bfloat16 [32768, 14848], P('gy', 'gx'), may hold values from -0.03125 to 0.03125
- kv_cache: bfloat16 [512, 4, 2, 256, 128], P('gy', 'gx'), may hold values from -300 to 300
- lengths: int32 [512], P('gy'), may hold values from 2 to 256, as said below
Outputs:
- block_out: bfloat16 [512, 14848], P('gy', 'gx')
Inputs may be any that keep to these rules, and one draw needn't show every extreme that they name: `lengths`: each sequence has 2 or more cached tokens, and one sequence exactly 256 in every draw.
All inputs are finite; a program needn't handle non-finite values.
Results may differ from a plain program's by a relative error of at most 0.005.
Values may be sent and summed in bfloat16 or wider, within the bound.
A program may use at most 128 MiB of HBM per device.

v0:
```python
import jax
import jax.numpy as jnp
from jax import lax
from jax.sharding import PartitionSpec as P


def attend(q_mine, kv_mine, cache, lengths):
    seqs = q_mine.shape[0]
    heads = q_mine.shape[2]
    head_dim = q_mine.shape[3]
    span = cache.shape[3]
    query = q_mine.reshape(seqs, 2, heads // 2, head_dim)
    fresh = kv_mine.reshape(seqs, 2, 2 * head_dim)
    local = cache[:, 0]
    keys = local[..., :head_dim]
    values = local[..., head_dim:]
    scores = jnp.einsum("bagd,bald->bagl", query, keys, preferred_element_type=jnp.float32) * 0.125
    valid = jnp.arange(span)[None, None, None, :] < lengths[:, None, None, None]
    scores = jnp.where(valid, scores, -1e30)
    score_new = (
        jnp.einsum(
            "bagd,bad->bag", query, fresh[..., :head_dim], preferred_element_type=jnp.float32
        )
        * 0.125
    )
    top = jnp.maximum(jnp.max(scores, axis=-1), score_new)
    expo = jnp.exp(scores - top[..., None])
    expo_new = jnp.exp(score_new - top)
    total = jnp.sum(expo, axis=-1) + expo_new
    weight = (expo / total[..., None]).astype(jnp.bfloat16)
    weight_new = (expo_new / total).astype(jnp.bfloat16)
    attended = jnp.einsum("bagl,bald->bagd", weight, values, preferred_element_type=jnp.float32)
    attended = attended + weight_new.astype(jnp.float32)[..., None] * fresh[
        :, :, None, head_dim:
    ].astype(jnp.float32)
    return attended.astype(jnp.bfloat16).reshape(seqs, 1, heads, head_dim)


def on_device(normed, residual, w_query, w_keyval, w_out, w_up, w_down, kv_cache, lengths):
    rows = normed.shape[0]
    width = normed.shape[1]
    slots = w_query.shape[2]
    head_dim = w_query.shape[3]
    kv_cols = w_keyval.shape[2]
    q_part = jnp.dot(normed, w_query.reshape(width, -1), preferred_element_type=jnp.float32)
    q_part = q_part.reshape(rows, 4, slots, head_dim)
    kv_part = jnp.dot(normed, w_keyval.reshape(width, -1), preferred_element_type=jnp.float32)
    kv_part = kv_part.reshape(rows, 4, kv_cols)
    up_part = jnp.dot(normed, w_up, preferred_element_type=jnp.float32)
    q_all, kv_all, up_all = lax.psum((q_part, kv_part, up_part), "gx")
    q_send = q_all.astype(jnp.bfloat16)
    kv_send = kv_all.astype(jnp.bfloat16).reshape(rows, 4, kv_cols, 1)
    hidden = jax.nn.gelu(up_all, approximate=False).astype(jnp.bfloat16)
    q_pairs, kv_pairs = (
        lax.all_to_all(q_send, "gy", split_axis=0, concat_axis=2, tiled=True),
        lax.all_to_all(kv_send, "gy", split_axis=0, concat_axis=2, tiled=True),
    )
    owner = lax.axis_index("gx")
    q_mine = lax.dynamic_slice_in_dim(q_pairs, owner, 1, 1)
    kv_mine = lax.dynamic_slice_in_dim(kv_pairs, owner, 1, 1)
    attended = attend(q_mine, kv_mine, kv_cache, lengths)
    returned = lax.all_to_all(attended, "gy", split_axis=2, concat_axis=0, tiled=True)
    heads_all = lax.all_gather(returned, "gx", axis=1, tiled=True)
    attn_part = jnp.einsum("bosd,sodn->bn", heads_all, w_out, preferred_element_type=jnp.float32)
    ffn_part = jnp.dot(hidden, w_down, preferred_element_type=jnp.float32)
    attn_rows, ffn_rows = (
        lax.psum_scatter(attn_part, "gy", scatter_dimension=0, tiled=True),
        lax.psum_scatter(ffn_part, "gy", scatter_dimension=0, tiled=True),
    )
    summed = attn_rows + ffn_rows
    return (residual.astype(jnp.float32) + summed).astype(jnp.bfloat16)


def solution(mesh):
    placed = (
        P(None, "gx"),
        P("gy", "gx"),
        P("gx", None, "gy", None),
        P("gx", None, "gy"),
        P("gy", None, None, "gx"),
        P("gx", "gy"),
        P("gy", "gx"),
        P("gy", "gx", None, None, None),
        P("gy"),
    )
    return jax.shard_map(
        on_device, mesh=mesh, in_specs=placed, out_specs=P("gy", "gx"), check_vma=False
    )
```

profile of v0, /device:TPU:0, one launch (start us, length us, event | category | flops | bytes accessed | tf_op | source)
XLA Modules:
  0.0 327.5 jit_solution(5859902660213113529)
XLA Ops:
  6.5 0.0 copy-start
  6.5 0.0 copy-start.4
  6.5 0.0 copy-start.5
  6.5 3.4 %fusion = f32[512,4,8]{0,2,1:T(8,128)S(1)} fusion(bf16[512,3712]{1,0:T(8,128)(2,1)} %param.9, bf16[3712,4,8]{0,2,1:T(8,128)(2,1)} %param.12), kind=kOutput, calls=%fused_computation.1 | convolution fusion | flops 121634816 | bytes 4104192 | tf_op jit(solution)/shard_map/dot_general | solution.py:47
  10.0 0.0 copy-done.4
  10.0 0.6 copy-done.5
  10.6 1.2 fusion.17
  11.8 22.1 %all-reduce.5 = (bf16[512,4,1,64]{0,3,1,2:T(8,128)(2,1)S(1)}, bf16[512,4,8]{0,2,1:T(8,128)(2,1)S(1)}) all-reduce(f32[512,4,1,64]{0,3,1,2:T(8,128)S(1)} %fusion.17, f32[512,4,8]{0,2,1:T(8,128)S(1)} %fusion), channel_id=1, replica_groups=mesh['gx'=4,'gy'=32] {'gx'}, use_global_device_ids=true, to_apply=%region_0.0 | all-reduce | flops 147456 | bytes 884736 | tf_op jit(solution)/shard_map/psum | solution.py:50
  33.8 0.3 copy.30
  34.2 1.2 reshape.76
  35.4 8.4 %all-to-all-start.1 = ((bf16[32,2,256]{2,1,0:T(2,128)(2,1)}), bf16[32,2,256]{2,1,0:T(2,128)(2,1)S(1)}, u32[]{:S(2)}, u32[]{:S(2)}) async-start(bf16[32,2,256]{2,1,0:T(2,128)(2,1)} %reshape.76), calls=%async_computation.1 | async-start | bytes 65536 | tf_op jit(solution)/shard_map/all_to_all | solution.py:56
  43.7 0.0 all-reduce.4.cloned.1.call-start
  43.8 9.8 %fusion.98 = f32[512,1024]{1,0:T(8,128)} fusion(bf16[512,3712]{1,0:T(8,128)(2,1)} %param.9, bf16[3712,1024]{1,0:T(8,128)(2,1)} %param.14), kind=kOutput, calls=%fused_computation.116 | convolution fusion | flops 3892314112 | bytes 13500416 | tf_op jit(solution)/shard_map/dot_general | solution.py:49
  53.6 0.0 copy-start.3
  53.6 0.0 all-reduce.4.cloned.1.call-update
  53.6 0.6 copy-done.3
  54.3 0.1 iota_compare_fusion
  54.3 0.3 copy.26
  54.7 1.1 reshape.74
  55.8 3.9 %copy.29 = bf16[16,1,2,256,128]{3,4,2,0,1:T(8,128)(2,1)} copy(bf16[16,1,2,256,128]{4,3,2,1,0:T(8,128)(2,1)} %param.16) | data formatting | bytes 4194304 | tf_op args[7]
  59.7 0.0 all-to-all-done.1
  59.7 8.3 %all-to-all-start = ((bf16[32,2,2048]{2,1,0:T(2,128)(2,1)}), bf16[32,2,2048]{2,1,0:T(2,128)(2,1)S(1)}, u32[]{:S(2)}, u32[]{:S(2)}) async-start(bf16[32,2,2048]{2,1,0:T(2,128)(2,1)} %reshape.74), calls=%async_computation | async-start | bytes 524288 | tf_op jit(solution)/shard_map/all_to_all | solution.py:55
  68.0 0.0 reduce-scatter.2.cloned.1.call-start
  68.0 0.6 reshape.77
  68.6 0.4 copy.39
  69.0 0.1 copy.42
  69.1 0.1 copy.41
  69.2 11.1 %all-to-all-done = bf16[32,2,2048]{2,1,0:T(2,128)(2,1)S(1)} async-done(((bf16[32,2,2048]{2,1,0:T(2,128)(2,1)}), bf16[32,2,2048]{2,1,0:T(2,128)(2,1)S(1)}, u32[]{:S(2)}, u32[]{:S(2)}) %all-to-all-start) | async-done | bytes 262176 | tf_op jit(solution)/shard_map/all_to_all | solution.py:55
  80.3 0.4 reshape.75
  80.7 0.0 copy-start.1
  80.7 0.1 copy.27
  80.8 0.2 fusion.62
  81.0 1.8 fusion.97
  82.8 0.3 fusion.57
  83.2 0.0 copy-done.1
  83.2 0.5 fusion.22
  83.6 0.1 copy.46
  83.7 0.1 reshape.78
  83.8 11.7 %all_to_all.48 = bf16[32,2,512]{2,1,0:T(2,128)(2,1)S(1)} all-to-all(bf16[32,2,512]{2,1,0:T(2,128)(2,1)S(1)} %reshape.78), channel_id=1, replica_groups=mesh['gx'=4,'gy'=32] {'gy'}, dimensions={0} | all-to-all | bytes 131072 | tf_op jit(solution)/shard_map/all_to_all | solution.py:62
  95.5 0.1 reshape.79
  95.6 0.1 copy.35
  95.7 9.0 %all_gather.3 = bf16[512,4,1,64]{0,3,2,1:T(8,128)(2,1)S(1)} all-gather(bf16[512,1,1,64]{0,3,2,1:T(8,128)(2,1)S(1)} %copy.35), channel_id=1, replica_groups=mesh['gx'=4,'gy'=32] {'gx'}, dimensions={1}, use_global_device_ids=true | all-gather | bytes 327680 | tf_op jit(solution)/shard_map/all_gather | solution.py:63
  104.7 12.5 %all-reduce.4.cloned.1.call-done = f32[512,1024]{1,0:T(8,128)} async-done(((f32[512,1024]{1,0:T(8,128)}), f32[512,1024]{1,0:T(8,128)}) %all-reduce.4.cloned.1.call-update) | async-done | bytes 2097168 | tf_op jit(solution)/shard_map/psum | solution.py:50
  117.3 12.3 %fusion.23 = f32[512,3712]{1,0:T(8,128)S(1)} fusion(bf16[1024,3712]{1,0:T(8,128)(2,1)} %param.15, f32[512,1024]{1,0:T(8,128)} %all-reduce.4.cloned.1.call-done), kind=kOutput, calls=%fused_computation.31 | convolution fusion | flops 3926392832 | bytes 17301504 | tf_op jit(solution)/shard_map/dot_general | solution.py:65
  129.6 0.0 copy-done
  129.6 4.3 %bitcast_add_fusion = f32[512,3712]{1,0:T(8,128)} fusion(f32[512,3712]{1,0:T(8,128)S(1)} %fusion.23, bf16[1,4,64,3712]{3,2,1,0:T(8,128)(2,1)S(1)} %copy-done, bf16[512,4,1,64]{0,3,2,1:T(8,128)(2,1)S(1)} %all_gather.3), kind=kOutput, calls=%fused_computation | convolution fusion | flops 974979072 | bytes 17367040 | tf_op jit(solution)/shard_map/bosd,sodn->bn/dot_general | solution.py:64
  134.0 0.0 copy-start.2
  134.0 0.0 reduce-scatter.2.cloned.1.call-update
  134.0 185.1 %reduce-scatter.2.cloned.1.call-done = f32[16,3712]{1,0:T(8,128)} async-done(((f32[512,3712]{1,0:T(8,128)}), f32[16,3712]{1,0:T(8,128)}) %reduce-scatter.2.cloned.1.call-update) | async-done | bytes 237584 | tf_op jit(solution)/shard_map/reduce_scatter | solution.py:67
  319.1 0.0 copy-done.2
  319.1 1.6 add_convert_fusion
  (7 shorter events, 0.1 us)
Async XLA Ops:
  6.5 123.1 %copy-start = (bf16[1,4,64,3712]{3,2,1,0:T(8,128)(2,1)S(1)}, bf16[1,4,64,3712]{3,2,1,0:T(8,128)(2,1)}, u32[]{:S(2)}) copy-start(bf16[1,4,64,3712]{3,2,1,0:T(8,128)(2,1)} %param.13) | copy-start | bytes 5701636
  6.5 3.4 %copy-start.4 = (bf16[512,3712]{1,0:T(8,128)(2,1)S(1)}, bf16[512,3712]{1,0:T(8,128)(2,1)}, u32[]{:S(2)}) copy-start(bf16[512,3712]{1,0:T(8,128)(2,1)} %param.9) | copy-start | bytes 11403268
  6.5 4.0 %copy-start.5 = (bf16[3712,4,1,64]{0,3,2,1:T(8,128)(2,1)S(1)}, bf16[3712,4,1,64]{0,3,2,1:T(8,128)(2,1)}, u32[]{:S(2)}) copy-start(bf16[3712,4,1,64]{0,3,2,1:T(8,128)(2,1)} %param.11) | copy-start | bytes 5701636
  35.4 24.3 %all-to-all-start.1 = ((bf16[32,2,256]{2,1,0:T(2,128)(2,1)}), bf16[32,2,256]{2,1,0:T(2,128)(2,1)S(1)}, u32[]{:S(2)}, u32[]{:S(2)}) async-start(bf16[32,2,256]{2,1,0:T(2,128)(2,1)} %reshape.76), calls=%async_computation.1 | async-start | bytes 65536 | tf_op jit(solution)/shard_map/all_to_all | solution.py:56
  43.7 73.6 %all-reduce.4.cloned.1.call-start = ((), (), s32[]{:S(2)}) async-start(), calls=%async_computation.4 | async-start | bytes 4194304 | tf_op jit(solution)/shard_map/psum | solution.py:50
  53.6 0.7 copy-start.3
  59.7 20.7 %all-to-all-start = ((bf16[32,2,2048]{2,1,0:T(2,128)(2,1)}), bf16[32,2,2048]{2,1,0:T(2,128)(2,1)S(1)}, u32[]{:S(2)}, u32[]{:S(2)}) async-start(bf16[32,2,2048]{2,1,0:T(2,128)(2,1)} %reshape.74), calls=%async_computation | async-start | bytes 524288 | tf_op jit(solution)/shard_map/all_to_all | solution.py:55
  68.0 251.1 %reduce-scatter.2.cloned.1.call-start = ((), (), s32[]{:S(2)}) async-start(), calls=%async_computation.5 | async-start | bytes 7839744 | tf_op jit(solution)/shard_map/reduce_scatter | solution.py:67
  80.7 2.5 copy-start.1
  134.0 185.1 %copy-start.2 = (bf16[16,3712]{1,0:T(8,128)(2,1)S(1)}, bf16[16,3712]{1,0:T(8,128)(2,1)}, u32[]{:S(2)}) copy-start(bf16[16,3712]{1,0:T(8,128)(2,1)} %param.10) | copy-start | bytes 356356
Sparse Core Ops, SparseCore 0:
  53.8 63.4 all-reduce.3
  134.1 184.9 reduce-scatter.1
where the time goes:
time: 328 us
  waiting for transfers between devices  209 us (64%)
  blocking collectives  42.7 us (13%)
  matrix products  33.5 us (10%)
  starting transfers between devices  16.7 us (5%)
  between operations  13.6 us (4%)
  local copies, waits for them, and re-layouts  10.1 us (3%)
    reduce_scatter x1, waiting for transfers between devices, on_device(): lax.psum_scatter(attn_part, 'gy', scatter_dimension=0, tiled=True)  185 us
    psum x1, blocking collectives, on_device(): q_all, kv_all, up_all = lax.psum((q_part, kv_part, up_part), 'gx')  22.1 us
    psum x1, waiting for transfers between devices, on_device(): q_all, kv_all, up_all = lax.psum((q_part, kv_part, up_part), 'gx')  12.5 us
    dot_general x1, matrix products, on_device(): ffn_part = jnp.dot(hidden, w_down, preferred_element_type=jnp.float32)  12.3 us
    all_to_all x1, blocking collectives, on_device(): lax.all_to_all(attended, 'gy', split_axis=2, concat_axis=0, tiled=True)  11.7 us
    all_to_all x1, waiting for transfers between devices, on_device(): lax.all_to_all(q_send, 'gy', split_axis=0, concat_axis=2, tiled=True)  11.1 us
    dot_general x1, matrix products, on_device(): up_part = jnp.dot(normed, w_up, preferred_element_type=jnp.float32)  9.84 us
    all_gather x1, blocking collectives, on_device(): heads_all = lax.all_gather(returned, 'gx', axis=1, tiled=True)  9.02 us
  transfers between devices with their start and end apart: 4, of which 3 were waited for; matrix products, arithmetic and copies ran while one was open for 6% of the time, Pallas kernels for 0%

commit v1 on v0

--- a/solution.py
+++ b/solution.py
@@ -1,7 +1,218 @@
+import functools
+
 import jax
 import jax.numpy as jnp
 from jax import lax
+from jax.experimental import pallas as pl
+from jax.experimental.pallas import tpu as pltpu
 from jax.sharding import PartitionSpec as P
+
+
+MESH = pl.DeviceIdType.MESH
+
+
+def cdot(a, b):
+    return lax.dot_general(a, b, (((1,), (0,)), ((), ())), preferred_element_type=jnp.float32)
+
+
+def column_chunks(width, lanes):
+    tiles = width // 128
+    first = (tiles // 2) // 2 * 2
+    cols = []
+    for lo, hi in ((0, first * 128), (first * 128, width)):
+        parts = []
+        while lo < hi:
+            w = min(lanes, hi - lo)
+            parts.append((lo, w))
+            lo += w
+        cols.append(parts)
+    order = []
+    for i in range(max(len(cols[0]), len(cols[1]))):
+        for s in (0, 1):
+            if i < len(cols[s]):
+                order.append((s, cols[s][i][0], cols[s][i][1]))
+    return order
+
+
+def down_kernel(chunks, hid_ref, heads_ref, wd_hbm, wo_hbm, out_ref, wd, wo, part, r1, s1, part2, r2, s2, part3, own3, r3,
+                wsem, ssem, rsem):
+    gx = lax.axis_index("gx")
+    gy = lax.axis_index("gy")
+    y, z, xl = gy // 8, (gy // 2) % 4, gy % 2
+
+    def at(yy, zz, xx):
+        return (gx, (yy * 4 + zz) * 2 + xx)
+
+    ring = (
+        (at((y + 1) % 4, z, xl), at((y + 3) % 4, z, xl)),
+        (at(y, (z + 1) % 4, xl), at(y, (z + 3) % 4, xl)),
+    )
+    pair = at(y, z, 1 - xl)
+    coord = (y, z)
+
+    loads = []
+    for k, (_, c, w) in enumerate(chunks):
+        cols = pl.ds(c, w)
+        a = pltpu.make_async_copy(wd_hbm.at[:, cols], wd.at[:, cols], wsem.at[2 * k])
+        b = pltpu.make_async_copy(wo_hbm.at[:, cols], wo.at[:, cols], wsem.at[2 * k + 1])
+        a.start()
+        b.start()
+        loads.append((a, b))
+
+    barrier = pltpu.get_barrier_semaphore()
+    for dev in ring[0] + ring[1] + (pair,):
+        pl.semaphore_signal(barrier, inc=1, device_id=dev, device_id_type=MESH)
+    pl.semaphore_wait(barrier, 5)
+
+    copies = {}
+
+    def send(k, i, src, dst, dev):
+        cp = pltpu.make_async_remote_copy(
+            src_ref=src, dst_ref=dst, send_sem=ssem.at[k, i], recv_sem=rsem.at[k, i], device_id=dev, device_id_type=MESH
+        )
+        cp.start()
+        copies[k, i] = cp
+
+    def f32(v):
+        return v.astype(jnp.float32)
+
+    def step_compute(k):
+        s, c, w = chunks[k]
+        cols = pl.ds(c, w)
+        p = coord[s]
+        plus, minus = ring[s]
+        for ld in loads[k]:
+            ld.wait()
+        acc = cdot(hid_ref[...], wd[:, cols]) + cdot(heads_ref[...], wo[:, cols])
+        acc = acc.astype(jnp.bfloat16)
+        for i in range(4):
+            for j in range(4):
+                row = (i * 4 + j) * 32
+                if s == 0:
+                    part[i, j, :, cols] = acc[row : row + 32]
+                else:
+                    part[j, i, :, cols] = acc[row : row + 32]
+        far, nxt, prv = (p + 2) % 4, (p + 1) % 4, (p + 3) % 4
+        send(k, 0, part.at[far, 0:2, :, cols], r1.at[0, :, :, cols], plus)
+        send(k, 1, part.at[far, 2:4, :, cols], r1.at[1, :, :, cols], minus)
+        send(k, 2, part.at[nxt, 2:4, :, cols], r1.at[2, :, :, cols], plus)
+        send(k, 3, part.at[prv, 0:2, :, cols], r1.at[3, :, :, cols], minus)
+
+    def step_relay1(k):
+        s, c, w = chunks[k]
+        cols = pl.ds(c, w)
+        p = coord[s]
+        plus, minus = ring[s]
+        nxt, prv = (p + 1) % 4, (p + 3) % 4
+        copies[k, 0].wait_recv()
+        s1[0, :, :, cols] = (f32(r1[0, :, :, cols]) + f32(part[nxt, 0:2, :, cols])).astype(jnp.bfloat16)
+        send(k, 4, s1.at[0, :, :, cols], r1.at[4, :, :, cols], plus)
+        copies[k, 1].wait_recv()
+        s1[1, :, :, cols] = (f32(r1[1, :, :, cols]) + f32(part[prv, 2:4, :, cols])).astype(jnp.bfloat16)
+        send(k, 5, s1.at[1, :, :, cols], r1.at[5, :, :, cols], minus)
+
+    def step_second(k):
+        s, c, w = chunks[k]
+        cols = pl.ds(c, w)
+        p, q = coord[s], coord[1 - s]
+        plus, minus = ring[1 - s]
+        copies[k, 2].wait_recv()
+        copies[k, 3].wait_recv()
+        copies[k, 4].wait_recv()
+        a = f32(part[p, 0:2, :, cols]) + f32(r1[4, :, :, cols]) + f32(r1[3, :, :, cols])
+        part2[0:2, :, cols] = a.astype(jnp.bfloat16)
+        copies[k, 5].wait_recv()
+        b = f32(part[p, 2:4, :, cols]) + f32(r1[5, :, :, cols]) + f32(r1[2, :, :, cols])
+        part2[2:4, :, cols] = b.astype(jnp.bfloat16)
+        far, nxt, prv = (q + 2) % 4, (q + 1) % 4, (q + 3) % 4
+        send(k, 6, part2.at[far, 0:16, cols], r2.at[0, :, cols], plus)
+        send(k, 7, part2.at[far, 16:32, cols], r2.at[1, :, cols], minus)
+        send(k, 8, part2.at[nxt, 16:32, cols], r2.at[2, :, cols], plus)
+        send(k, 9, part2.at[prv, 0:16, cols], r2.at[3, :, cols], minus)
+
+    def step_relay2(k):
+        s, c, w = chunks[k]
+        cols = pl.ds(c, w)
+        q = coord[1 - s]
+        plus, minus = ring[1 - s]
+        nxt, prv = (q + 1) % 4, (q + 3) % 4
+        copies[k, 6].wait_recv()
+        s2[0, :, cols] = (f32(r2[0, :, cols]) + f32(part2[nxt, 0:16, cols])).astype(jnp.bfloat16)
+        send(k, 10, s2.at[0, :, cols], r2.at[4, :, cols], plus)
+        copies[k, 7].wait_recv()
+        s2[1, :, cols] = (f32(r2[1, :, cols]) + f32(part2[prv, 16:32, cols])).astype(jnp.bfloat16)
+        send(k, 11, s2.at[1, :, cols], r2.at[5, :, cols], minus)
+
+    def step_pair(k):
+        s, c, w = chunks[k]
+        cols = pl.ds(c, w)
+        q = coord[1 - s]
+        for i in (8, 9, 10, 11):
+            copies[k, i].wait_recv()
+        a = f32(part2[q, 0:16, cols]) + f32(r2[4, :, cols]) + f32(r2[3, :, cols])
+        b = f32(part2[q, 16:32, cols]) + f32(r2[5, :, cols]) + f32(r2[2, :, cols])
+        part3[0, :, cols] = a.astype(jnp.bfloat16)
+        part3[1, :, cols] = b.astype(jnp.bfloat16)
+        own3[0, :, cols] = a
+        own3[1, :, cols] = b
+        send(k, 12, part3.at[1 - xl, :, cols], r3.at[:, cols], pair)
+
+    def step_last(k):
+        s, c, w = chunks[k]
+        cols = pl.ds(c, w)
+        copies[k, 12].wait_recv()
+        out_ref[:, cols] = own3[xl, :, cols] + f32(r3[:, cols])
+
+    steps = (step_compute, step_relay1, step_second, step_relay2, step_pair, step_last)
+    lag = (0, 1, 2, 3, 4, 5)
+    n = len(chunks)
+    for t in range(n + lag[-1]):
+        for fn, d in zip(steps, lag):
+            if 0 <= t - d < n:
+                fn(t - d)
+    for k in range(n):
+        for i in range(13):
+            copies[k, i].wait_send()
+
+
+def down_and_scatter(hidden, heads, w_down, w_out, lanes=512):
+    width = w_down.shape[1]
+    chunks = column_chunks(width, lanes)
+    n = len(chunks)
+    bf = jnp.bfloat16
+    return pl.pallas_call(
+        functools.partial(down_kernel, chunks),
+        out_shape=jax.ShapeDtypeStruct((16, width), jnp.float32),
+        in_specs=[
+            pl.BlockSpec(memory_space=pltpu.VMEM),
+            pl.BlockSpec(memory_space=pltpu.VMEM),
+            pl.BlockSpec(memory_space=pl.ANY),
+            pl.BlockSpec(memory_space=pl.ANY),
+        ],
+        out_specs=pl.BlockSpec(memory_space=pltpu.VMEM),
+        scratch_shapes=[
+            pltpu.VMEM(w_down.shape, bf),
+            pltpu.VMEM(w_out.shape, bf),
+            pltpu.VMEM((4, 4, 32, width), bf),
+            pltpu.VMEM((6, 2, 32, width), bf),
+            pltpu.VMEM((2, 2, 32, width), bf),
+            pltpu.VMEM((4, 32, width), bf),
+            pltpu.VMEM((6, 16, width), bf),
+            pltpu.VMEM((2, 16, width), bf),
+            pltpu.VMEM((2, 16, width), bf),
+            pltpu.VMEM((2, 16, width), jnp.float32),
+            pltpu.VMEM((16, width), bf),
+            pltpu.SemaphoreType.DMA((2 * n,)),
+            pltpu.SemaphoreType.DMA((n, 13)),
+            pltpu.SemaphoreType.DMA((n, 13)),
+        ],
+        compiler_params=pltpu.CompilerParams(
+            collective_id=1, has_side_effects=True, vmem_limit_bytes=56 * 1024 * 1024
+        ),
+        cost_estimate=pl.CostEstimate(
+            flops=2 * 512 * 1280 * width, bytes_accessed=2 * 1280 * width, transcendentals=0
+        ),
+    )(hidden, heads, w_down, w_out)
 
 
 def attend(q_mine, kv_mine, cache, lengths):
@@ -61,13 +272,9 @@
     attended = attend(q_mine, kv_mine, kv_cache, lengths)
     returned = lax.all_to_all(attended, "gy", split_axis=2, concat_axis=0, tiled=True)
     heads_all = lax.all_gather(returned, "gx", axis=1, tiled=True)
-    attn_part = jnp.einsum("bosd,sodn->bn", heads_all, w_out, preferred_element_type=jnp.float32)
-    ffn_part = jnp.dot(hidden, w_down, preferred_element_type=jnp.float32)
-    attn_rows, ffn_rows = (
-        lax.psum_scatter(attn_part, "gy", scatter_dimension=0, tiled=True),
-        lax.psum_scatter(ffn_part, "gy", scatter_dimension=0, tiled=True),
-    )
-    summed = attn_rows + ffn_rows
+    summed = down_and_scatter(
+        hidden, heads_all.reshape(rows, -1), w_down, w_out.reshape(-1, w_out.shape[3])
+    )
     return (residual.astype(jnp.float32) + summed).astype(jnp.bfloat16)
 
 

time: 328 us -> 178 us (0.54)
  waiting for transfers between devices: 209 us -> 22.9 us
  Pallas kernels: 0 us -> 44.9 us
  matrix products: 33.5 us -> 16.8 us
  other arithmetic: 2.04 us -> 8.6 us
    reduce_scatter x1 -> x0, waiting for transfers between devices: 185 us -> none  [on_device(): lax.psum_scatter(attn_part, 'gy', scatter_dimension=0, tiled=True)]
    pallas_call x0 -> x1, Pallas kernels: none -> 44.9 us  [down_and_scatter(): pl.pallas_call(functools.partial(down_kernel, chunks), out_shape=jax.Shap...]
    dot_general x2 -> x0, matrix products: 16.7 us -> none  [the longest x1 12.3 us: on_device(): ffn_part = jnp.dot(hidden, w_down, preferred_element_type=jnp.float32)]
    convert_element_type x0 -> x1, other arithmetic: none -> 6.57 us  [on_device(): hidden = jax.nn.gelu(up_all, approximate=False).astype(jnp.bfloat16)]
    unnamed x21 -> x19, local copies, waits for them, and re-layouts: 8.83 us -> 8.68 us
  transfers between devices with their start and end apart: 4 -> 3, of which waited for: 3 -> 2; matrix products, arithmetic and copies ran while one was open for 6% -> 12% of each run, Pallas kernels for 0% -> 0%
where the time goes in v1:
time: 178 us; the launch traced here: 177 us
  Pallas kernels  44.9 us (25%)
  blocking collectives  42.8 us (24%)
  waiting for transfers between devices  22.9 us (13%)
  matrix products  16.8 us (9%)
  starting transfers between devices  16.7 us (9%)
  between operations  13.6 us (8%)
  local copies, waits for them, and re-layouts  10.8 us (6%)
  other arithmetic  8.6 us (5%)
    pallas_call x1, Pallas kernels, down_and_scatter(): pl.pallas_call(functools.partial(down_kernel, chunks), out_shape=jax.Shap...  44.9 us
    psum x1, blocking collectives, on_device(): q_all, kv_all, up_all = lax.psum((q_part, kv_part, up_part), 'gx')  22.1 us
    psum x1, waiting for transfers between devices, on_device(): q_all, kv_all, up_all = lax.psum((q_part, kv_part, up_part), 'gx')  11.7 us
    all_to_all x1, blocking collectives, on_device(): lax.all_to_all(attended, 'gy', split_axis=2, concat_axis=0, tiled=True)  11.7 us
    all_to_all x1, waiting for transfers between devices, on_device(): lax.all_to_all(q_send, 'gy', split_axis=0, concat_axis=2, tiled=True)  11.2 us
    dot_general x1, matrix products, on_device(): up_part = jnp.dot(normed, w_up, preferred_element_type=jnp.float32)  9.84 us
    all_gather x1, blocking collectives, on_device(): heads_all = lax.all_gather(returned, 'gx', axis=1, tiled=True)  9.02 us
    unnamed x19, local copies, waits for them, and re-layouts  8.68 us
  transfers between devices with their start and end apart: 3, of which 2 were waited for; matrix products, arithmetic and copies ran while one was open for 12% of the time, Pallas kernels for 0%

profile of v1, /device:TPU:0, one launch (start us, length us, event | category | flops | bytes accessed | tf_op | source)
XLA Modules:
  0.0 177.1 jit_solution(12671195947126444550)
XLA Ops:
  6.5 0.0 copy-start
  6.5 0.0 copy-start.4
  6.5 3.4 %fusion = f32[512,4,8]{0,2,1:T(8,128)S(1)} fusion(bf16[512,3712]{1,0:T(8,128)(2,1)} %param.9, bf16[3712,4,8]{0,2,1:T(8,128)(2,1)} %param.12), kind=kOutput, calls=%fused_computation | convolution fusion | flops 121634816 | bytes 4104192 | tf_op jit(solution)/shard_map/dot_general | solution.py:258
  10.0 0.0 copy-done
  10.0 0.4 copy-done.4
  10.4 1.2 fusion.16
  11.6 22.1 %all-reduce.5 = (bf16[512,4,1,64]{0,3,1,2:T(8,128)(2,1)S(1)}, bf16[512,4,8]{0,2,1:T(8,128)(2,1)S(1)}) all-reduce(f32[512,4,1,64]{0,3,1,2:T(8,128)S(1)} %fusion.16, f32[512,4,8]{0,2,1:T(8,128)S(1)} %fusion), channel_id=1, replica_groups=mesh['gx'=4,'gy'=32] {'gx'}, use_global_device_ids=true, to_apply=%region_1.0 | all-reduce | flops 147456 | bytes 884736 | tf_op jit(solution)/shard_map/psum | solution.py:261
  33.7 0.3 copy.32
  34.0 1.2 reshape.75
  35.2 8.4 %all-to-all-start.1 = ((bf16[32,2,256]{2,1,0:T(2,128)(2,1)}), bf16[32,2,256]{2,1,0:T(2,128)(2,1)S(1)}, u32[]{:S(2)}, u32[]{:S(2)}) async-start(bf16[32,2,256]{2,1,0:T(2,128)(2,1)} %reshape.75), calls=%async_computation.1 | async-start | bytes 65536 | tf_op jit(solution)/shard_map/all_to_all | solution.py:267
  43.6 0.0 all-reduce.4.cloned.1.call-start
  43.6 9.8 %fusion.34 = f32[512,1024]{1,0:T(8,128)} fusion(bf16[512,3712]{1,0:T(8,128)(2,1)} %param.9, bf16[3712,1024]{1,0:T(8,128)(2,1)} %param.14), kind=kOutput, calls=%fused_computation.52 | convolution fusion | flops 3892314112 | bytes 13500416 | tf_op jit(solution)/shard_map/dot_general | solution.py:260
  53.4 0.0 copy-start.3
  53.4 0.0 all-reduce.4.cloned.1.call-update
  53.5 0.6 copy-done.3
  54.1 0.1 iota_compare_fusion
  54.2 0.3 copy.28
  54.5 1.1 reshape.73
  55.6 3.9 %copy.31 = bf16[16,1,2,256,128]{3,4,2,0,1:T(8,128)(2,1)} copy(bf16[16,1,2,256,128]{4,3,2,1,0:T(8,128)(2,1)} %param.16) | data formatting | bytes 4194304 | tf_op args[7]
  59.5 0.0 all-to-all-done.1
  59.5 8.3 %all-to-all-start = ((bf16[32,2,2048]{2,1,0:T(2,128)(2,1)}), bf16[32,2,2048]{2,1,0:T(2,128)(2,1)S(1)}, u32[]{:S(2)}, u32[]{:S(2)}) async-start(bf16[32,2,2048]{2,1,0:T(2,128)(2,1)} %reshape.73), calls=%async_computation | async-start | bytes 524288 | tf_op jit(solution)/shard_map/all_to_all | solution.py:266
  67.8 0.6 reshape.76
  68.4 0.4 copy.42
  68.8 0.1 copy.45
  68.9 0.1 copy.44
  69.0 11.2 %all-to-all-done = bf16[32,2,2048]{2,1,0:T(2,128)(2,1)S(1)} async-done(((bf16[32,2,2048]{2,1,0:T(2,128)(2,1)}), bf16[32,2,2048]{2,1,0:T(2,128)(2,1)S(1)}, u32[]{:S(2)}, u32[]{:S(2)}) %all-to-all-start) | async-done | bytes 262176 | tf_op jit(solution)/shard_map/all_to_all | solution.py:266
  80.2 0.4 reshape.74
  80.5 0.0 copy-start.1
  80.6 0.1 copy.29
  80.7 0.2 fusion.28
  80.9 1.8 %fusion.33 = (f32[16,2,16]{2,1,0:T(2,128)S(1)}, f32[16,2,16,256]{3,2,1,0:T(8,128)S(1)}) fusion(bf16[16,2,16,64]{3,2,1,0:T(8,128)(2,1)S(1)} %bitcast.73, bf16[16,2,256,128]{2,3,1,0:T(8,128)(2,1)} %bitcast.62, pred[16,256]{1,0:T(8,128)(4,1)S(1)} %iota_compare_fusion), kind=kOutput, calls=%fused_computation.50 | convolution fusion | flops 17169920 | bytes 1644544 | tf_op jit(solution)/shard_map/bagd,bald->bagl/dot_general | solution.py:228
  82.7 0.3 fusion.24
  83.0 0.0 copy-done.1
  83.0 0.5 fusion.21
  83.5 0.1 copy.49
  83.5 0.1 reshape.77
  83.7 11.7 %all_to_all.48 = bf16[32,2,512]{2,1,0:T(2,128)(2,1)S(1)} all-to-all(bf16[32,2,512]{2,1,0:T(2,128)(2,1)S(1)} %reshape.77), channel_id=1, replica_groups=mesh['gx'=4,'gy'=32] {'gy'}, dimensions={0} | all-to-all | bytes 131072 | tf_op jit(solution)/shard_map/all_to_all | solution.py:273
  95.3 0.1 reshape.78
  95.5 0.1 copy.37
  95.6 9.0 %all_gather.3 = bf16[512,4,1,64]{0,3,2,1:T(8,128)(2,1)S(1)} all-gather(bf16[512,1,1,64]{0,3,2,1:T(8,128)(2,1)S(1)} %copy.37), channel_id=1, replica_groups=mesh['gx'=4,'gy'=32] {'gx'}, dimensions={1}, use_global_device_ids=true | all-gather | bytes 327680 | tf_op jit(solution)/shard_map/all_gather | solution.py:274
  104.6 0.8 copy.38.heads_ref
  105.4 11.7 %all-reduce.4.cloned.1.call-done = f32[512,1024]{1,0:T(8,128)} async-done(((f32[512,1024]{1,0:T(8,128)}), f32[512,1024]{1,0:T(8,128)}) %all-reduce.4.cloned.1.call-update) | async-done | bytes 2097168 | tf_op jit(solution)/shard_map/psum | solution.py:261
  117.1 6.6 %fusion.6.hid_ref = bf16[512,1024]{1,0:T(8,128)(2,1)} fusion(f32[512,1024]{1,0:T(8,128)} %all-reduce.4.cloned.1.call-done), kind=kLoop, calls=%fused_computation.7 | loop fusion | flops 34078720 | bytes 3145728 | tf_op jit(solution)/shard_map/convert_element_type | solution.py:264
  123.7 0.0 copy-start.2
  123.7 44.9 %shard_map.91 = f32[16,3712]{1,0:T(8,128)} custom-call(bf16[512,1024]{1,0:T(8,128)(2,1)} %fusion.6.hid_ref, bf16[512,256]{1,0:T(8,128)(2,1)} %copy.38.heads_ref, bf16[1024,3712]{1,0:T(8,128)(2,1)} %wd_hbm.1, bf16[256,3712]{1,0:T(8,128)(2,1)} %bitcast.81), custom_call_target="tpu_custom_call" | custom-call | flops 4865392640 | bytes 9502720 | tf_op jit(solution)/shard_map/pallas_call | solution.py:183
  168.6 0.0 copy-done.2
  168.6 1.6 add_convert_fusion
  (7 shorter events, 0.1 us)
Async XLA Ops:
  6.5 3.4 %copy-start = (bf16[3712,4,1,64]{0,3,2,1:T(8,128)(2,1)S(1)}, bf16[3712,4,1,64]{0,3,2,1:T(8,128)(2,1)}, u32[]{:S(2)}) copy-start(bf16[3712,4,1,64]{0,3,2,1:T(8,128)(2,1)} %param.11) | copy-start | bytes 5701636
  6.5 3.9 %copy-start.4 = (bf16[512,3712]{1,0:T(8,128)(2,1)S(1)}, bf16[512,3712]{1,0:T(8,128)(2,1)}, u32[]{:S(2)}) copy-start(bf16[512,3712]{1,0:T(8,128)(2,1)} %param.9) | copy-start | bytes 11403268
  35.2 24.3 %all-to-all-start.1 = ((bf16[32,2,256]{2,1,0:T(2,128)(2,1)}), bf16[32,2,256]{2,1,0:T(2,128)(2,1)S(1)}, u32[]{:S(2)}, u32[]{:S(2)}) async-start(bf16[32,2,256]{2,1,0:T(2,128)(2,1)} %reshape.75), calls=%async_computation.1 | async-start | bytes 65536 | tf_op jit(solution)/shard_map/all_to_all | solution.py:267
  43.6 73.6 %all-reduce.4.cloned.1.call-start = ((), (), s32[]{:S(2)}) async-start(), calls=%async_computation.3 | async-start | bytes 4194304 | tf_op jit(solution)/shard_map/psum | solution.py:261
  53.4 0.7 copy-start.3
  59.5 20.7 %all-to-all-start = ((bf16[32,2,2048]{2,1,0:T(2,128)(2,1)}), bf16[32,2,2048]{2,1,0:T(2,128)(2,1)S(1)}, u32[]{:S(2)}, u32[]{:S(2)}) async-start(bf16[32,2,2048]{2,1,0:T(2,128)(2,1)} %reshape.73), calls=%async_computation | async-start | bytes 524288 | tf_op jit(solution)/shard_map/all_to_all | solution.py:266
  80.5 2.5 %copy-start.1 = (bf16[16,1,2,256,128]{3,4,2,0,1:T(8,128)(2,1)S(1)}, bf16[16,1,2,256,128]{3,4,2,0,1:T(8,128)(2,1)}, u32[]{:S(2)}) copy-start(bf16[16,1,2,256,128]{3,4,2,0,1:T(8,128)(2,1)} %copy.31) | copy-start | bytes 6291460
  123.7 44.9 %copy-start.2 = (bf16[16,3712]{1,0:T(8,128)(2,1)S(1)}, bf16[16,3712]{1,0:T(8,128)(2,1)}, u32[]{:S(2)}) copy-start(bf16[16,3712]{1,0:T(8,128)(2,1)} %param.10) | copy-start | bytes 356356
Sparse Core Ops, SparseCore 0:
  53.6 63.4 all-reduce.3

commit v2 on v1

--- a/solution.py
+++ b/solution.py
@@ -6,7 +6,6 @@
 from jax.experimental import pallas as pl
 from jax.experimental.pallas import tpu as pltpu
 from jax.sharding import PartitionSpec as P
-
 
 MESH = pl.DeviceIdType.MESH
 
@@ -215,66 +214,285 @@
     )(hidden, heads, w_down, w_out)
 
 
-def attend(q_mine, kv_mine, cache, lengths):
-    seqs = q_mine.shape[0]
-    heads = q_mine.shape[2]
-    head_dim = q_mine.shape[3]
-    span = cache.shape[3]
-    query = q_mine.reshape(seqs, 2, heads // 2, head_dim)
-    fresh = kv_mine.reshape(seqs, 2, 2 * head_dim)
-    local = cache[:, 0]
-    keys = local[..., :head_dim]
-    values = local[..., head_dim:]
-    scores = jnp.einsum("bagd,bald->bagl", query, keys, preferred_element_type=jnp.float32) * 0.125
-    valid = jnp.arange(span)[None, None, None, :] < lengths[:, None, None, None]
-    scores = jnp.where(valid, scores, -1e30)
-    score_new = (
-        jnp.einsum(
-            "bagd,bad->bag", query, fresh[..., :head_dim], preferred_element_type=jnp.float32
+def tdot(a, b):
+    return lax.dot_general(a, b, (((1,), (1,)), ((), ())), preferred_element_type=jnp.float32)
+
+
+def iotas(shape):
+    return lax.broadcasted_iota(jnp.int32, shape, 0), lax.broadcasted_iota(jnp.int32, shape, 1)
+
+
+def one_hot(mask):
+    return jnp.where(mask, 1.0, 0.0).astype(jnp.bfloat16)
+
+
+def front_kernel(len_ref, x_hbm, wq_hbm, wkv_hbm, wu_hbm, kv_hbm, hid_out, heads_out, xv, wq, wkv, wu, kv, qpart, qr1, qs, qr2,
+                 qa, qrecv, us, ur, xs, ux, own, hid, perm, iperm, ss, wv, att, asend, hrecv, heads4, wsem, ssem, rsem, asem, brecv):
+    bf = jnp.bfloat16
+    gx = lax.axis_index("gx")
+    gy = lax.axis_index("gy")
+    xh, c = gx // 2, gx % 2
+    core = (xh * 2 + 1 - c, gy)
+    far = ((1 - xh) * 2 + c, gy)
+    order = ((1 - xh) * 2 + 1 - c, (1 - xh) * 2 + c, xh * 2 + 1 - c, gx)
+
+    def quarter(g):
+        return pl.ds(pl.multiple_of(g * 256, 256), 256)
+
+    loads = [
+        pltpu.make_async_copy(x_hbm, xv, wsem.at[0]),
+        pltpu.make_async_copy(wq_hbm, wq, wsem.at[1]),
+        pltpu.make_async_copy(wkv_hbm, wkv, wsem.at[2]),
+    ]
+    for i in range(4):
+        loads.append(pltpu.make_async_copy(wu_hbm.at[:, quarter(order[i])], wu.at[i], wsem.at[3 + i]))
+    loads.append(pltpu.make_async_copy(kv_hbm, kv, wsem.at[7]))
+    for ld in loads:
+        ld.start()
+
+    barrier = pltpu.get_barrier_semaphore()
+    pl.semaphore_signal(barrier, inc=1, device_id=core, device_id_type=MESH)
+    pl.semaphore_signal(barrier, inc=1, device_id=far, device_id_type=MESH)
+
+    def greet(i, carry):
+        pl.semaphore_signal(barrier, inc=1, device_id=(gx, (gy + i) % 32), device_id_type=MESH)
+        return carry
+
+    lax.fori_loop(1, 32, greet, 0)
+
+    r, k = iotas((512, 512))
+    perm[...] = one_hot(k == (r % 32) * 16 + r // 32)
+    iperm[...] = one_hot(k == (r % 16) * 32 + r // 16)
+
+    pl.semaphore_wait(barrier, 33)
+
+    copies = {}
+
+    def send(i, src, dst, dev):
+        cp = pltpu.make_async_remote_copy(
+            src_ref=src, dst_ref=dst, send_sem=ssem.at[i], recv_sem=rsem.at[i], device_id=dev, device_id_type=MESH
         )
-        * 0.125
-    )
-    top = jnp.maximum(jnp.max(scores, axis=-1), score_new)
-    expo = jnp.exp(scores - top[..., None])
-    expo_new = jnp.exp(score_new - top)
-    total = jnp.sum(expo, axis=-1) + expo_new
-    weight = (expo / total[..., None]).astype(jnp.bfloat16)
-    weight_new = (expo_new / total).astype(jnp.bfloat16)
-    attended = jnp.einsum("bagl,bald->bagd", weight, values, preferred_element_type=jnp.float32)
-    attended = attended + weight_new.astype(jnp.float32)[..., None] * fresh[
-        :, :, None, head_dim:
-    ].astype(jnp.float32)
-    return attended.astype(jnp.bfloat16).reshape(seqs, 1, heads, head_dim)
+        cp.start()
+        copies[i] = cp
+
+    for ld in loads[:3]:
+        ld.wait()
+    qt = tdot(wq[...], xv[...])
+    kvt = tdot(wkv[...], xv[...])
+    for o in range(4):
+        qpart[o // 2, o % 2, 0:64, :] = qt[o * 64 : o * 64 + 64]
+        qpart[o // 2, o % 2, 64:72, :] = kvt[o * 8 : o * 8 + 8]
+    send(0, qpart.at[1 - xh, 1 - c], qr1.at[0], core)
+    send(1, qpart.at[xh, 1 - c], qr1.at[1], core)
+
+    loads[3].wait()
+    us[0] = cdot(xv[...], wu[0]).astype(bf)
+    send(2, us.at[0], ur.at[0], core)
+
+    copies[0].wait_recv()
+    qs[...] = qpart[1 - xh, c] + qr1[0]
+    send(3, qs, qr2, far)
+
+    loads[4].wait()
+    up = cdot(xv[...], wu[1])
+    copies[2].wait_recv()
+    xs[...] = (up + ur[0].astype(jnp.float32)).astype(bf)
+    send(4, xs.at[0:256], ux.at[0:256], far)
+    send(5, xs.at[256:512], ux.at[256:512], far)
+
+    loads[5].wait()
+    us[1] = cdot(xv[...], wu[2]).astype(bf)
+    send(6, us.at[1], ur.at[1], core)
+
+    copies[1].wait_recv()
+    copies[3].wait_recv()
+    qsum = qpart[xh, c] + qr1[1] + qr2[...]
+    qrows = jnp.concatenate([qsum, jnp.zeros((56, 512), jnp.float32)], axis=0).T
+    qa[...] = qrows.astype(bf).reshape(32, 16, 128)
+    qrecv[gy] = qa[gy]
+
+    def hop(which, src, dst):
+        def body(i, carry):
+            peer = (gy + i) % 32
+            pltpu.make_async_remote_copy(
+                src_ref=src.at[peer],
+                dst_ref=dst.at[gy],
+                send_sem=asem.at[which, i],
+                recv_sem=brecv.at[which, i],
+                device_id=(gx, peer),
+                device_id_type=MESH,
+            ).start()
+            return carry
+
+        lax.fori_loop(1, 32, body, 0)
+
+    def hop_copy(which, src, dst, i):
+        peer = (gy + i) % 32
+        return pltpu.make_async_remote_copy(
+            src_ref=src.at[peer],
+            dst_ref=dst.at[(gy + 32 - i) % 32],
+            send_sem=asem.at[which, i],
+            recv_sem=brecv.at[which, i],
+            device_id=(gx, peer),
+            device_id_type=MESH,
+        )
+
+    def hop_recv(which, src, dst):
+        def body(i, carry):
+            hop_copy(which, src, dst, i).wait_recv()
+            return carry
+
+        lax.fori_loop(1, 32, body, 0)
+
+    def hop_sent(which, src, dst):
+        def body(i, carry):
+            hop_copy(which, src, dst, i).wait_send()
+            return carry
+
+        lax.fori_loop(1, 32, body, 0)
+
+    hop(0, qa, qrecv)
+
+    loads[6].wait()
+    own[...] = cdot(xv[...], wu[3])
+    copies[6].wait_recv()
+    own[...] += ur[1].astype(jnp.float32)
+    loads[7].wait()
+
+    hop_recv(0, qa, qrecv)
+    qall = qrecv[...].reshape(512, 128)
+    k2, j2 = iotas((128, 256))
+    spread = cdot(qall, one_hot(k2 - 64 == j2 % 8))
+    r3, j3 = iotas((512, 256))
+    spread = jnp.where(j3 // 8 == r3 // 16, spread, 0.0).astype(bf)
+    b4, r4 = iotas((16, 512))
+    fresh = cdot(one_hot(r4 % 16 == b4), spread).astype(bf)
+    fr = jnp.concatenate([fresh[:, 0:128], fresh[:, 128:256]], axis=0)
+    qp = cdot(perm[...], qall)
+    _, lane = iotas((512, 128))
+    q128 = jnp.where(lane < 64, qp, 0.0).astype(bf)
+    _, pos = iotas((16, 256))
+    for b in range(16):
+        ln = len_ref[b]
+        for a in range(2):
+            row = b * 32 + a * 16
+            sc = tdot(q128[row : row + 16], kv[b, a]) * 0.125
+            ss[row : row + 16, :] = jnp.where(pos < ln, sc, -1e30)
+    sn = tdot(q128, fr) * 0.125
+    r5, j5 = iotas((512, 32))
+    match = j5 == ((r5 // 16) % 2) * 16 + r5 // 32
+    sn = jnp.sum(jnp.where(match, sn, 0.0), axis=1, keepdims=True)
+    wns = []
+    for i in range(4):
+        blk = ss[i * 128 : (i + 1) * 128, :]
+        new = sn[i * 128 : (i + 1) * 128]
+        top = jnp.maximum(jnp.max(blk, axis=1, keepdims=True), new)
+        e = jnp.exp(blk - top)
+        en = jnp.exp(new - top)
+        tot = jnp.sum(e, axis=1, keepdims=True) + en
+        wv[i * 128 : (i + 1) * 128, :] = (e / tot).astype(bf)
+        wns.append(en / tot)
+    wn = jnp.concatenate(wns, axis=0)
+    wnm = jnp.where(match, wn, 0.0).astype(bf)
+    for b in range(16):
+        for a in range(2):
+            row = b * 32 + a * 16
+            att[row : row + 16, :] = cdot(wv[row : row + 16, :], kv[b, a])
+    atted = (att[...] + cdot(wnm, fr)).astype(bf)
+    asend[...] = cdot(iperm[...], atted).astype(bf).reshape(32, 16, 128)
+    hrecv[gy] = asend[gy]
+    hop(1, asend, hrecv)
+
+    for h in range(2):
+        rows = slice(h * 256, h * 256 + 256)
+        copies[4 + h].wait_recv()
+        v = own[rows, :] + ux[rows, :].astype(jnp.float32)
+        v = 0.5 * v * (1.0 + lax.erf(v * 0.7071067811865476))
+        hid[rows, quarter(gx)] = v.astype(bf)
+        send(7 + h, hid.at[rows, quarter(gx)], hid.at[rows, quarter(gx)], far)
+        send(9 + h, hid.at[rows, quarter(gx)], hid.at[rows, quarter(gx)], core)
+
+    hop_recv(1, asend, hrecv)
+    heads4[gx] = hrecv[...].reshape(512, 128)
+    send(11, heads4.at[gx], heads4.at[gx], far)
+    send(12, heads4.at[gx], heads4.at[gx], core)
+
+    g = (1 - xh) * 2 + c
+    for h in range(2):
+        rows = slice(h * 256, h * 256 + 256)
+        copies[7 + h].wait_recv()
+        send(13 + h, hid.at[rows, quarter(g)], hid.at[rows, quarter(g)], core)
+    copies[11].wait_recv()
+    send(15, heads4.at[g], heads4.at[g], core)
+    copies[12].wait_recv()
+    for i in (9, 10, 13, 14, 15):
+        copies[i].wait_recv()
+    heads_out[...] = jnp.concatenate([heads4[o][:, 64:128] for o in range(4)], axis=1)
+    hid_out[...] = hid[...]
+    for i in range(16):
+        copies[i].wait_send()
+    hop_sent(0, qa, qrecv)
+    hop_sent(1, asend, hrecv)
+
+
+def front(normed, w_query, w_keyval, w_up, kv_cache, lengths):
+    width = normed.shape[1]
+    bf, f4 = jnp.bfloat16, jnp.float32
+    V = pltpu.VMEM
+    wq = jnp.transpose(w_query, (1, 2, 3, 0)).reshape(-1, width)
+    wkv = jnp.transpose(w_keyval, (1, 2, 0)).reshape(-1, width)
+    kv = kv_cache.reshape(16, 2, 256, 128)
+    hbm = pl.BlockSpec(memory_space=pl.ANY)
+    vm = pl.BlockSpec(memory_space=pltpu.VMEM)
+    return pl.pallas_call(
+        front_kernel,
+        out_shape=(jax.ShapeDtypeStruct((512, 1024), bf), jax.ShapeDtypeStruct((512, 256), bf)),
+        in_specs=[pl.BlockSpec(memory_space=pltpu.SMEM)] + [hbm] * 5,
+        out_specs=(vm, vm),
+        scratch_shapes=[
+            V((512, width), bf),
+            V((256, width), bf),
+            V((32, width), bf),
+            V((4, width, 256), bf),
+            V((16, 2, 256, 128), bf),
+            V((2, 2, 72, 512), f4),
+            V((2, 72, 512), f4),
+            V((72, 512), f4),
+            V((72, 512), f4),
+            V((32, 16, 128), bf),
+            V((32, 16, 128), bf),
+            V((2, 512, 256), bf),
+            V((2, 512, 256), bf),
+            V((512, 256), bf),
+            V((512, 256), bf),
+            V((512, 256), f4),
+            V((512, 1024), bf),
+            V((512, 512), bf),
+            V((512, 512), bf),
+            V((512, 256), f4),
+            V((512, 256), bf),
+            V((512, 128), f4),
+            V((32, 16, 128), bf),
+            V((32, 16, 128), bf),
+            V((4, 512, 128), bf),
+            pltpu.SemaphoreType.DMA((8,)),
+            pltpu.SemaphoreType.DMA((16,)),
+            pltpu.SemaphoreType.DMA((16,)),
+            pltpu.SemaphoreType.DMA((2, 32)),
+            pltpu.SemaphoreType.DMA((2, 32)),
+        ],
+        compiler_params=pltpu.CompilerParams(
+            collective_id=2, has_side_effects=True, vmem_limit_bytes=56 * 1024 * 1024
+        ),
+        cost_estimate=pl.CostEstimate(
+            flops=2 * 512 * 1312 * width, bytes_accessed=2 * 1824 * width, transcendentals=0
+        ),
+    )(lengths, normed, wq, wkv, w_up, kv)
 
 
 def on_device(normed, residual, w_query, w_keyval, w_out, w_up, w_down, kv_cache, lengths):
-    rows = normed.shape[0]
-    width = normed.shape[1]
-    slots = w_query.shape[2]
-    head_dim = w_query.shape[3]
-    kv_cols = w_keyval.shape[2]
-    q_part = jnp.dot(normed, w_query.reshape(width, -1), preferred_element_type=jnp.float32)
-    q_part = q_part.reshape(rows, 4, slots, head_dim)
-    kv_part = jnp.dot(normed, w_keyval.reshape(width, -1), preferred_element_type=jnp.float32)
-    kv_part = kv_part.reshape(rows, 4, kv_cols)
-    up_part = jnp.dot(normed, w_up, preferred_element_type=jnp.float32)
-    q_all, kv_all, up_all = lax.psum((q_part, kv_part, up_part), "gx")
-    q_send = q_all.astype(jnp.bfloat16)
-    kv_send = kv_all.astype(jnp.bfloat16).reshape(rows, 4, kv_cols, 1)
-    hidden = jax.nn.gelu(up_all, approximate=False).astype(jnp.bfloat16)
-    q_pairs, kv_pairs = (
-        lax.all_to_all(q_send, "gy", split_axis=0, concat_axis=2, tiled=True),
-        lax.all_to_all(kv_send, "gy", split_axis=0, concat_axis=2, tiled=True),
-    )
-    owner = lax.axis_index("gx")
-    q_mine = lax.dynamic_slice_in_dim(q_pairs, owner, 1, 1)
-    kv_mine = lax.dynamic_slice_in_dim(kv_pairs, owner, 1, 1)
-    attended = attend(q_mine, kv_mine, kv_cache, lengths)
-    returned = lax.all_to_all(attended, "gy", split_axis=2, concat_axis=0, tiled=True)
-    heads_all = lax.all_gather(returned, "gx", axis=1, tiled=True)
-    summed = down_and_scatter(
-        hidden, heads_all.reshape(rows, -1), w_down, w_out.reshape(-1, w_out.shape[3])
-    )
+    hidden, heads = front(normed, w_query, w_keyval, w_up, kv_cache, lengths)
+    summed = down_and_scatter(hidden, heads, w_down, w_out.reshape(-1, w_out.shape[3]))
     return (residual.astype(jnp.float32) + summed).astype(jnp.bfloat16)
 
 

time: 178 us -> 93.9 us (0.53)
  Pallas kernels: 44.9 us -> 92 us
  blocking collectives: 42.8 us -> 0 us
  waiting for transfers between devices: 22.9 us -> 0 us
  matrix products: 16.8 us -> 0 us
  starting transfers between devices: 16.7 us -> 0 us
  between operations: 13.6 us -> 0.03 us
  local copies, waits for them, and re-layouts: 10.8 us -> 0.01 us
  other arithmetic: 8.6 us -> 1.61 us
    pallas_call x0 -> x1, Pallas kernels: none -> 46.2 us  [front(): pl.pallas_call(front_kernel, out_shape=(jax.ShapeDtypeStruct((512, 1024),...]
    psum x1 -> x0, blocking collectives: 22.1 us -> none  [on_device(): q_all, kv_all, up_all = lax.psum((q_part, kv_part, up_part), 'gx')]
    dot_general x6 -> x0, matrix products: 16.8 us -> none  [the longest x1 9.84 us: on_device(): up_part = jnp.dot(normed, w_up, preferred_element_type=jnp.float32)]
    all_to_all x2 -> x0, starting transfers between devices: 16.6 us -> none  [the longest x1 8.36 us: on_device(): lax.all_to_all(kv_send, 'gy', split_axis=0, concat_axis=2, tiled=True)]
    psum x1 -> x0, waiting for transfers between devices: 11.7 us -> none  [on_device(): q_all, kv_all, up_all = lax.psum((q_part, kv_part, up_part), 'gx')]
    all_to_all x1 -> x0, blocking collectives: 11.7 us -> none  [on_device(): lax.all_to_all(attended, 'gy', split_axis=2, concat_axis=0, tiled=True)]
    all_to_all x2 -> x0, waiting for transfers between devices: 11.2 us -> none  [the longest x1 11.2 us: on_device(): lax.all_to_all(q_send, 'gy', split_axis=0, concat_axis=2, tiled=True)]
    all_gather x1 -> x0, blocking collectives: 9.02 us -> none  [on_device(): heads_all = lax.all_gather(returned, 'gx', axis=1, tiled=True)]
  transfers between devices with their start and end apart: 3 -> 0, of which waited for: 2 -> 0; matrix products, arithmetic and copies ran while one was open for 12% -> 0% of each run, Pallas kernels for 0% -> 0%
where the time goes in v2:
time: 93.9 us; the launch traced here: 93.6 us
  Pallas kernels  92 us (98%)
  other arithmetic  1.61 us (2%)
    pallas_call x1, Pallas kernels, front(): pl.pallas_call(front_kernel, out_shape=(jax.ShapeDtypeStruct((512, 1024),...  46.2 us
    pallas_call x1, Pallas kernels, down_and_scatter(): pl.pallas_call(functools.partial(down_kernel, chunks), out_shape=jax.Shap...  45.8 us

profile of v2, /device:TPU:0, one launch (start us, length us, event | category | flops | bytes accessed | tf_op | source)
XLA Modules:
  0.0 93.6 jit_solution(4748153980677345076)
XLA Ops:
  0.0 46.2 %shard_map.91 = (bf16[512,1024]{1,0:T(8,128)(2,1)}, bf16[512,256]{1,0:T(8,128)(2,1)}) custom-call(s32[16]{0:T(128)} %len_ref.1, bf16[512,3712]{1,0:T(8,128)(2,1)} %x_hbm.1, bf16[256,3712]{1,0:T(8,128)(2,1)} %bitcast.9, bf16[32,3712]{1,0:T(8,128)(2,1)} %bitcast.11, bf16[3712,1024]{1,0:T(8,128)(2,1)} %wu_hbm.1, bf16[16,2,256,128]{3,2,1,0:T(8,128)(2,1)} %bitcast.8), custom_call_target="tpu_custom_call" | custom-call | flops 4987027456 | bytes 13541376 | tf_op jit(solution)/shard_map/pallas_call | solution.py:447
  46.2 0.0 copy-start
  46.2 45.8 %shard_map.92 = f32[16,3712]{1,0:T(8,128)} custom-call(bf16[512,1024]{1,0:T(8,128)(2,1)} %get-tuple-element.7.hid_ref, bf16[512,256]{1,0:T(8,128)(2,1)} %get-tuple-element.8.heads_ref, bf16[1024,3712]{1,0:T(8,128)(2,1)} %wd_hbm.1, bf16[256,3712]{1,0:T(8,128)(2,1)} %bitcast.10), custom_call_target="tpu_custom_call" | custom-call | flops 4865392640 | bytes 9502720 | tf_op jit(solution)/shard_map/pallas_call | solution.py:182
  92.0 0.0 copy-done
  92.0 1.6 %add_convert_fusion = bf16[16,3712]{1,0:T(8,128)(2,1)} fusion(f32[16,3712]{1,0:T(8,128)} %shard_map.92, bf16[16,3712]{1,0:T(8,128)(2,1)S(1)} %copy-done), kind=kLoop, calls=%fused_computation | loop fusion | flops 178176 | bytes 475136 | tf_op jit(solution)/shard_map/convert_element_type | solution.py:496
Async XLA Ops:
  46.2 45.8 %copy-start = (bf16[16,3712]{1,0:T(8,128)(2,1)S(1)}, bf16[16,3712]{1,0:T(8,128)(2,1)}, u32[]{:S(2)}) copy-start(bf16[16,3712]{1,0:T(8,128)(2,1)} %param.10) | copy-start | bytes 356356

commit v3 on v1

v3 whole, which is shorter than its diff:
```python
import functools

import jax
import jax.numpy as jnp
from jax import lax
from jax.experimental import pallas as pl
from jax.experimental.pallas import tpu as pltpu
from jax.sharding import PartitionSpec as P

MESH = pl.DeviceIdType.MESH


def cdot(a, b):
    return lax.dot_general(a, b, (((1,), (0,)), ((), ())), preferred_element_type=jnp.float32)


def column_chunks(width, lanes):
    tiles = width // 128
    first = (tiles // 2) // 2 * 2
    cols = []
    for lo, hi in ((0, first * 128), (first * 128, width)):
        parts = []
        while lo < hi:
            w = min(lanes, hi - lo)
            parts.append((lo, w))
            lo += w
        cols.append(parts)
    order = []
    for i in range(max(len(cols[0]), len(cols[1]))):
        for s in (0, 1):
            if i < len(cols[s]):
                order.append((s, cols[s][i][0], cols[s][i][1]))
    return order


def tdot(a, b):
    return lax.dot_general(a, b, (((1,), (1,)), ((), ())), preferred_element_type=jnp.float32)


def iotas(shape):
    return lax.broadcasted_iota(jnp.int32, shape, 0), lax.broadcasted_iota(jnp.int32, shape, 1)


def one_hot(mask):
    return jnp.where(mask, 1.0, 0.0).astype(jnp.bfloat16)


def layer_kernel(chunks, lag, len_ref, x_hbm, wq_hbm, wkv_hbm, wu_hbm, kv_hbm, wd_hbm, wo_hbm, out_ref,
                 xv, wq, wkv, wu, kv, qpart, qr1, qs, qr2, qa, qrecv, us, ur, xs, ux, own, act, perm, iperm, ss, wv, att, asend,
                 hrecv, heads4, wd, part, r1, s1, part2, r2, s2, part3, own3, r3, wsem, fsend, frecv, asem, brecv, ssem, rsem):
    bf = jnp.bfloat16
    gx = lax.axis_index("gx")
    gy = lax.axis_index("gy")
    xh, c = gx // 2, gx % 2
    y, z, xl = gy // 8, (gy // 2) % 4, gy % 2
    core = (xh * 2 + 1 - c, gy)
    far = ((1 - xh) * 2 + c, gy)
    order = ((1 - xh) * 2 + 1 - c, (1 - xh) * 2 + c, xh * 2 + 1 - c, gx)

    def f32(v):
        return v.astype(jnp.float32)

    def quarter(g):
        return pl.ds(pl.multiple_of(g * 256, 256), 256)

    loads = [
        pltpu.make_async_copy(x_hbm, xv, wsem.at[0]),
        pltpu.make_async_copy(wq_hbm, wq, wsem.at[1]),
        pltpu.make_async_copy(wkv_hbm, wkv, wsem.at[2]),
    ]
    for i in range(4):
        loads.append(pltpu.make_async_copy(wu_hbm.at[:, quarter(order[i])], wu.at[i], wsem.at[3 + i]))
    loads.append(pltpu.make_async_copy(kv_hbm, kv, wsem.at[7]))
    for ld in loads:
        ld.start()
    late = []
    for k, (_, lo, w) in enumerate(chunks):
        cols = pl.ds(lo, w)
        late.append(
            (
                pltpu.make_async_copy(wd_hbm.at[:, cols], wd.at[0:1024, cols], wsem.at[8 + 2 * k]),
                pltpu.make_async_copy(wo_hbm.at[:, cols], wd.at[1024:1280, cols], wsem.at[9 + 2 * k]),
            )
        )

    barrier = pltpu.get_barrier_semaphore()
    pl.semaphore_signal(barrier, inc=1, device_id=core, device_id_type=MESH)
    pl.semaphore_signal(barrier, inc=1, device_id=far, device_id_type=MESH)

    def greet(i, carry):
        pl.semaphore_signal(barrier, inc=1, device_id=(gx, (gy + i) % 32), device_id_type=MESH)
        return carry

    lax.fori_loop(1, 32, greet, 0)

    moved = {}

    def move(i, src, dst, dev):
        cp = pltpu.make_async_remote_copy(
            src_ref=src, dst_ref=dst, send_sem=fsend.at[i], recv_sem=frecv.at[i], device_id=dev, device_id_type=MESH
        )
        cp.start()
        moved[i] = cp

    for ld in loads[:3]:
        ld.wait()
    qt = tdot(wq[...], xv[...])
    kvt = tdot(wkv[...], xv[...])
    for o in range(4):
        qpart[o // 2, o % 2, 0:64, :] = qt[o * 64 : o * 64 + 64]
        qpart[o // 2, o % 2, 64:72, :] = kvt[o * 8 : o * 8 + 8]
    pl.semaphore_wait(barrier, 33)
    move(0, qpart.at[1 - xh, 1 - c], qr1.at[0], core)
    move(1, qpart.at[xh, 1 - c], qr1.at[1], core)

    loads[3].wait()
    us[0] = cdot(xv[...], wu[0]).astype(bf)
    move(2, us.at[0], ur.at[0], core)

    moved[0].wait_recv()
    qs[...] = qpart[1 - xh, c] + qr1[0]
    move(3, qs, qr2, far)

    loads[4].wait()
    up = cdot(xv[...], wu[1])
    moved[2].wait_recv()
    xs[...] = (up + f32(ur[0])).astype(bf)
    for h in range(4):
        rows = slice(h * 128, h * 128 + 128)
        move(4 + h, xs.at[rows], ux.at[rows], far)

    for a, b in late:
        a.start()
        b.start()

    loads[5].wait()
    us[1] = cdot(xv[...], wu[2]).astype(bf)
    move(8, us.at[1], ur.at[1], core)

    r, k = iotas((512, 512))
    perm[...] = one_hot(k == (r % 32) * 16 + r // 32)
    iperm[...] = one_hot(k == (r % 16) * 32 + r // 16)

    moved[1].wait_recv()
    moved[3].wait_recv()
    qsum = qpart[xh, c] + qr1[1] + qr2[...]
    qrows = jnp.concatenate([qsum, jnp.zeros((56, 512), jnp.float32)], axis=0).T
    qa[...] = qrows.astype(bf).reshape(32, 16, 128)
    qrecv[gy] = qa[gy]

    def hop_copy(which, src, dst, i, slot):
        peer = (gy + i) % 32
        return pltpu.make_async_remote_copy(
            src_ref=src.at[peer],
            dst_ref=dst.at[slot],
            send_sem=asem.at[which, i],
            recv_sem=brecv.at[which, i],
            device_id=(gx, peer),
            device_id_type=MESH,
        )

    def hop(which, src, dst):
        def body(i, carry):
            hop_copy(which, src, dst, i, gy).start()
            return carry

        lax.fori_loop(1, 32, body, 0)

    def hop_recv(which, src, dst):
        def body(i, carry):
            hop_copy(which, src, dst, i, (gy + 32 - i) % 32).wait_recv()
            return carry

        lax.fori_loop(1, 32, body, 0)

    def hop_sent(which, src, dst):
        def body(i, carry):
            hop_copy(which, src, dst, i, gy).wait_send()
            return carry

        lax.fori_loop(1, 32, body, 0)

    hop(0, qa, qrecv)

    loads[6].wait()
    own[...] = cdot(xv[...], wu[3])
    moved[8].wait_recv()
    own[...] += f32(ur[1])

    def gelu_rows(h):
        rows = slice(h * 128, h * 128 + 128)
        moved[4 + h].wait_recv()
        v = own[rows, :] + f32(ux[rows, :])
        v = 0.5 * v * (1.0 + lax.erf(v * 0.7071067811865476))
        act[rows, quarter(gx)] = v.astype(bf)
        here = act.at[rows, quarter(gx)]
        move(9 + h, here, here, far)
        move(13 + h, here, here, core)

    gelu_rows(0)
    gelu_rows(1)

    loads[7].wait()
    hop_recv(0, qa, qrecv)
    qall = qrecv[...].reshape(512, 128)
    k2, j2 = iotas((128, 256))
    spread = cdot(qall, one_hot(k2 - 64 == j2 % 8))
    e3, j3 = iotas((512, 256))
    spread = jnp.where(j3 // 8 == e3 // 16, spread, 0.0).astype(bf)
    b4, e4 = iotas((16, 512))
    fresh = cdot(one_hot(e4 % 16 == b4), spread).astype(bf)
    fr = jnp.concatenate([fresh[:, 0:128], fresh[:, 128:256]], axis=0)
    qp = cdot(perm[...], qall)
    _, lane = iotas((512, 128))
    q128 = jnp.where(lane < 64, qp, 0.0).astype(bf)
    _, pos = iotas((16, 256))
    for b in range(16):
        ln = len_ref[b]
        for a in range(2):
            row = b * 32 + a * 16
            sc = tdot(q128[row : row + 16], kv[b, a]) * 0.125
            ss[row : row + 16, :] = jnp.where(pos < ln, sc, -1e30)
    sn = tdot(q128, fr) * 0.125
    e5, j5 = iotas((512, 32))
    match = j5 == ((e5 // 16) % 2) * 16 + e5 // 32
    sn = jnp.sum(jnp.where(match, sn, 0.0), axis=1, keepdims=True)
    wns = []
    for i in range(4):
        blk = ss[i * 128 : (i + 1) * 128, :]
        new = sn[i * 128 : (i + 1) * 128]
        top = jnp.maximum(jnp.max(blk, axis=1, keepdims=True), new)
        e = jnp.exp(blk - top)
        en = jnp.exp(new - top)
        tot = jnp.sum(e, axis=1, keepdims=True) + en
        wv[i * 128 : (i + 1) * 128, :] = (e / tot).astype(bf)
        wns.append(en / tot)
    wn = jnp.concatenate(wns, axis=0)
    wnm = jnp.where(match, wn, 0.0).astype(bf)
    for b in range(16):
        for a in range(2):
            row = b * 32 + a * 16
            att[row : row + 16, :] = cdot(wv[row : row + 16, :], kv[b, a])
    atted = (att[...] + cdot(wnm, fr)).astype(bf)
    asend[...] = cdot(iperm[...], atted).astype(bf).reshape(32, 16, 128)
    hrecv[gy] = asend[gy]
    hop(1, asend, hrecv)


    gelu_rows(2)
    gelu_rows(3)

    g = (1 - xh) * 2 + c

    def pass_on(h):
        rows = slice(h * 128, h * 128 + 128)
        moved[9 + h].wait_recv()
        there = act.at[rows, quarter(g)]
        move(17 + h, there, there, core)

    pass_on(0)
    pass_on(1)
    hop_recv(1, asend, hrecv)
    hr = hrecv[...].reshape(512, 128)
    heads4[gx] = jnp.concatenate([hr[0:256, 64:128], hr[256:512, 64:128]], axis=1)
    move(21, heads4.at[gx], heads4.at[gx], far)
    move(22, heads4.at[gx], heads4.at[gx], core)
    pass_on(2)
    pass_on(3)
    moved[21].wait_recv()
    move(23, heads4.at[g], heads4.at[g], core)
    moved[22].wait_recv()
    for i in range(13, 21):
        moved[i].wait_recv()
    moved[23].wait_recv()
    for h in range(2):
        act[h * 256 : h * 256 + 256, 1024:1280] = jnp.concatenate(
            [heads4[o][:, h * 64 : h * 64 + 64] for o in range(4)], axis=1
        )

    def at(yy, zz, xx):
        return (gx, (yy * 4 + zz) * 2 + xx)

    ring = (
        (at((y + 1) % 4, z, xl), at((y + 3) % 4, z, xl)),
        (at(y, (z + 1) % 4, xl), at(y, (z + 3) % 4, xl)),
    )
    pair = at(y, z, 1 - xl)
    coord = (y, z)

    copies = {}

    def send(k, i, src, dst, dev):
        cp = pltpu.make_async_remote_copy(
            src_ref=src, dst_ref=dst, send_sem=ssem.at[k, i], recv_sem=rsem.at[k, i], device_id=dev, device_id_type=MESH
        )
        cp.start()
        copies[k, i] = cp

    def step_compute(k):
        s, lo, w = chunks[k]
        cols = pl.ds(lo, w)
        p = coord[s]
        plus, minus = ring[s]
        for ld in late[k]:
            ld.wait()
        acc = cdot(act[...], wd[:, cols])
        acc = acc.astype(jnp.bfloat16)
        for i in range(4):
            for j in range(4):
                row = (i * 4 + j) * 32
                if s == 0:
                    part[i, j, :, cols] = acc[row : row + 32]
                else:
                    part[j, i, :, cols] = acc[row : row + 32]
        far, nxt, prv = (p + 2) % 4, (p + 1) % 4, (p + 3) % 4
        send(k, 0, part.at[far, 0:2, :, cols], r1.at[0, :, :, cols], plus)
        send(k, 1, part.at[far, 2:4, :, cols], r1.at[1, :, :, cols], minus)
        send(k, 2, part.at[nxt, 2:4, :, cols], r1.at[2, :, :, cols], plus)
        send(k, 3, part.at[prv, 0:2, :, cols], r1.at[3, :, :, cols], minus)

    def step_relay1(k):
        s, lo, w = chunks[k]
        cols = pl.ds(lo, w)
        p = coord[s]
        plus, minus = ring[s]
        nxt, prv = (p + 1) % 4, (p + 3) % 4
        copies[k, 0].wait_recv()
        s1[0, :, :, cols] = (f32(r1[0, :, :, cols]) + f32(part[nxt, 0:2, :, cols])).astype(jnp.bfloat16)
        send(k, 4, s1.at[0, :, :, cols], r1.at[4, :, :, cols], plus)
        copies[k, 1].wait_recv()
        s1[1, :, :, cols] = (f32(r1[1, :, :, cols]) + f32(part[prv, 2:4, :, cols])).astype(jnp.bfloat16)
        send(k, 5, s1.at[1, :, :, cols], r1.at[5, :, :, cols], minus)

    def step_second(k):
        s, lo, w = chunks[k]
        cols = pl.ds(lo, w)
        p, q = coord[s], coord[1 - s]
        plus, minus = ring[1 - s]
        copies[k, 2].wait_recv()
        copies[k, 3].wait_recv()
        copies[k, 4].wait_recv()
        a = f32(part[p, 0:2, :, cols]) + f32(r1[4, :, :, cols]) + f32(r1[3, :, :, cols])
        part2[0:2, :, cols] = a.astype(jnp.bfloat16)
        copies[k, 5].wait_recv()
        b = f32(part[p, 2:4, :, cols]) + f32(r1[5, :, :, cols]) + f32(r1[2, :, :, cols])
        part2[2:4, :, cols] = b.astype(jnp.bfloat16)
        far, nxt, prv = (q + 2) % 4, (q + 1) % 4, (q + 3) % 4
        send(k, 6, part2.at[far, 0:16, cols], r2.at[0, :, cols], plus)
        send(k, 7, part2.at[far, 16:32, cols], r2.at[1, :, cols], minus)
        send(k, 8, part2.at[nxt, 16:32, cols], r2.at[2, :, cols], plus)
        send(k, 9, part2.at[prv, 0:16, cols], r2.at[3, :, cols], minus)

    def step_relay2(k):
        s, lo, w = chunks[k]
        cols = pl.ds(lo, w)
        q = coord[1 - s]
        plus, minus = ring[1 - s]
        nxt, prv = (q + 1) % 4, (q + 3) % 4
        copies[k, 6].wait_recv()
        s2[0, :, cols] = (f32(r2[0, :, cols]) + f32(part2[nxt, 0:16, cols])).astype(jnp.bfloat16)
        send(k, 10, s2.at[0, :, cols], r2.at[4, :, cols], plus)
        copies[k, 7].wait_recv()
        s2[1, :, cols] = (f32(r2[1, :, cols]) + f32(part2[prv, 16:32, cols])).astype(jnp.bfloat16)
        send(k, 11, s2.at[1, :, cols], r2.at[5, :, cols], minus)

    def step_pair(k):
        s, lo, w = chunks[k]
        cols = pl.ds(lo, w)
        q = coord[1 - s]
        for i in (8, 9, 10, 11):
            copies[k, i].wait_recv()
        a = f32(part2[q, 0:16, cols]) + f32(r2[4, :, cols]) + f32(r2[3, :, cols])
        b = f32(part2[q, 16:32, cols]) + f32(r2[5, :, cols]) + f32(r2[2, :, cols])
        part3[0, :, cols] = a.astype(jnp.bfloat16)
        part3[1, :, cols] = b.astype(jnp.bfloat16)
        own3[0, :, cols] = a
        own3[1, :, cols] = b
        send(k, 12, part3.at[1 - xl, :, cols], r3.at[:, cols], pair)

    def step_last(k):
        s, lo, w = chunks[k]
        cols = pl.ds(lo, w)
        copies[k, 12].wait_recv()
        out_ref[:, cols] = own3[xl, :, cols] + f32(r3[:, cols])

    steps = (step_compute, step_relay1, step_second, step_relay2, step_pair, step_last)
    n = len(chunks)
    for t in range(n + lag[-1]):
        for fn, d in zip(steps, lag):
            if 0 <= t - d < n:
                fn(t - d)
    for k in range(n):
        for i in range(13):
            copies[k, i].wait_send()
    for i in range(24):
        moved[i].wait_send()
    hop_sent(0, qa, qrecv)
    hop_sent(1, asend, hrecv)


def layer(normed, w_query, w_keyval, w_out, w_up, w_down, kv_cache, lengths, lanes=512, lag=(0, 2, 4, 6, 8, 10)):
    width = normed.shape[1]
    bf, f4 = jnp.bfloat16, jnp.float32
    V = pltpu.VMEM
    wq = jnp.transpose(w_query, (1, 2, 3, 0)).reshape(-1, width)
    wkv = jnp.transpose(w_keyval, (1, 2, 0)).reshape(-1, width)
    kv = kv_cache.reshape(16, 2, 256, 128)
    wo = w_out.reshape(-1, width)
    chunks = column_chunks(width, lanes)
    n = len(chunks)
    hbm = pl.BlockSpec(memory_space=pl.ANY)
    return pl.pallas_call(
        functools.partial(layer_kernel, chunks, lag),
        out_shape=jax.ShapeDtypeStruct((16, width), f4),
        in_specs=[pl.BlockSpec(memory_space=pltpu.SMEM)] + [hbm] * 7,
        out_specs=pl.BlockSpec(memory_space=pltpu.VMEM),
        scratch_shapes=[
            V((512, width), bf),
            V((256, width), bf),
            V((32, width), bf),
            V((4, width, 256), bf),
            V((16, 2, 256, 128), bf),
            V((2, 2, 72, 512), f4),
            V((2, 72, 512), f4),
            V((72, 512), f4),
            V((72, 512), f4),
            V((32, 16, 128), bf),
            V((32, 16, 128), bf),
            V((2, 512, 256), bf),
            V((2, 512, 256), bf),
            V((512, 256), bf),
            V((512, 256), bf),
            V((512, 256), f4),
            V((512, 1280), bf),
            V((512, 512), bf),
            V((512, 512), bf),
            V((512, 256), f4),
            V((512, 256), bf),
            V((512, 128), f4),
            V((32, 16, 128), bf),
            V((32, 16, 128), bf),
            V((4, 256, 128), bf),
            V((1280, width), bf),
            V((4, 4, 32, width), bf),
            V((6, 2, 32, width), bf),
            V((2, 2, 32, width), bf),
            V((4, 32, width), bf),
            V((6, 16, width), bf),
            V((2, 16, width), bf),
            V((2, 16, width), bf),
            V((2, 16, width), f4),
            V((16, width), bf),
            pltpu.SemaphoreType.DMA((8 + 2 * n,)),
            pltpu.SemaphoreType.DMA((24,)),
            pltpu.SemaphoreType.DMA((24,)),
            pltpu.SemaphoreType.DMA((2, 32)),
            pltpu.SemaphoreType.DMA((2, 32)),
            pltpu.SemaphoreType.DMA((n, 13)),
            pltpu.SemaphoreType.DMA((n, 13)),
        ],
        compiler_params=pltpu.CompilerParams(
            collective_id=1, has_side_effects=True, vmem_limit_bytes=60 * 1024 * 1024
        ),
        cost_estimate=pl.CostEstimate(
            flops=2 * 512 * 2592 * width, bytes_accessed=2 * 3200 * width, transcendentals=0
        ),
    )(lengths, normed, wq, wkv, w_up, kv, w_down, wo)


def on_device(normed, residual, w_query, w_keyval, w_out, w_up, w_down, kv_cache, lengths):
    summed = layer(normed, w_query, w_keyval, w_out, w_up, w_down, kv_cache, lengths)
    return (residual.astype(jnp.float32) + summed).astype(jnp.bfloat16)


def solution(mesh):
    placed = (
        P(None, "gx"),
        P("gy", "gx"),
        P("gx", None, "gy", None),
        P("gx", None, "gy"),
        P("gy", None, None, "gx"),
        P("gx", "gy"),
        P("gy", "gx"),
        P("gy", "gx", None, None, None),
        P("gy"),
    )
    return jax.shard_map(
        on_device, mesh=mesh, in_specs=placed, out_specs=P("gy", "gx"), check_vma=False
    )
```

time: 178 us -> 79.7 us (0.45)
  blocking collectives: 42.8 us -> 0 us
  Pallas kernels: 44.9 us -> 77.9 us
  waiting for transfers between devices: 22.9 us -> 0 us
  matrix products: 16.8 us -> 0 us
  starting transfers between devices: 16.7 us -> 0 us
  between operations: 13.6 us -> 0.02 us
  local copies, waits for them, and re-layouts: 10.8 us -> 0.01 us
  other arithmetic: 8.6 us -> 1.61 us
    pallas_call x1, Pallas kernels: 44.9 us -> 77.9 us  [layer(): pl.pallas_call(functools.partial(layer_kernel, chunks, lag), out_shape=ja...]
    psum x1 -> x0, blocking collectives: 22.1 us -> none  [on_device(): q_all, kv_all, up_all = lax.psum((q_part, kv_part, up_part), 'gx')]
    dot_general x6 -> x0, matrix products: 16.8 us -> none  [the longest x1 9.84 us: on_device(): up_part = jnp.dot(normed, w_up, preferred_element_type=jnp.float32)]
    all_to_all x2 -> x0, starting transfers between devices: 16.6 us -> none  [the longest x1 8.36 us: on_device(): lax.all_to_all(kv_send, 'gy', split_axis=0, concat_axis=2, tiled=True)]
    psum x1 -> x0, waiting for transfers between devices: 11.7 us -> none  [on_device(): q_all, kv_all, up_all = lax.psum((q_part, kv_part, up_part), 'gx')]
    all_to_all x1 -> x0, blocking collectives: 11.7 us -> none  [on_device(): lax.all_to_all(attended, 'gy', split_axis=2, concat_axis=0, tiled=True)]
    all_to_all x2 -> x0, waiting for transfers between devices: 11.2 us -> none  [the longest x1 11.2 us: on_device(): lax.all_to_all(q_send, 'gy', split_axis=0, concat_axis=2, tiled=True)]
    all_gather x1 -> x0, blocking collectives: 9.02 us -> none  [on_device(): heads_all = lax.all_gather(returned, 'gx', axis=1, tiled=True)]
  transfers between devices with their start and end apart: 3 -> 0, of which waited for: 2 -> 0; matrix products, arithmetic and copies ran while one was open for 12% -> 0% of each run, Pallas kernels for 0% -> 0%
where the time goes in v3:
time: 79.7 us; the launch traced here: 79.5 us
  Pallas kernels  77.9 us (98%)
  other arithmetic  1.61 us (2%)
    pallas_call x1, Pallas kernels, layer(): pl.pallas_call(functools.partial(layer_kernel, chunks, lag), out_shape=ja...  77.9 us
    convert_element_type x1, other arithmetic, on_device(): return (residual.astype(jnp.float32) + summed).astype(jnp.bfloat16)  1.61 us

profile of v3, /device:TPU:0, one launch (start us, length us, event | category | flops | bytes accessed | tf_op | source)
XLA Modules:
  0.0 79.5 jit_solution(13021488749260386986)
XLA Ops:
  0.0 0.0 copy-start
  0.0 77.9 %shard_map.91 = f32[16,3712]{1,0:T(8,128)} custom-call(s32[16]{0:T(128)} %len_ref.1, bf16[512,3712]{1,0:T(8,128)(2,1)} %x_hbm.1, bf16[256,3712]{1,0:T(8,128)(2,1)} %bitcast.9, bf16[32,3712]{1,0:T(8,128)(2,1)} %bitcast.11, bf16[3712,1024]{1,0:T(8,128)(2,1)} %wu_hbm.1, bf16[16,2,256,128]{3,2,1,0:T(8,128)(2,1)} %bitcast.8, bf16[1024,3712]{1,0:T(8,128)(2,1)} %wd_hbm.1, ...), custom_call_target="tpu_custom_call" | custom-call | flops 9852420096 | bytes 23756800 | tf_op jit(solution)/shard_map/pallas_call | solution.py:412
  77.9 0.0 copy-done
  77.9 1.6 %add_convert_fusion = bf16[16,3712]{1,0:T(8,128)(2,1)} fusion(f32[16,3712]{1,0:T(8,128)} %shard_map.91, bf16[16,3712]{1,0:T(8,128)(2,1)S(1)} %copy-done), kind=kLoop, calls=%fused_computation | loop fusion | flops 178176 | bytes 475136 | tf_op jit(solution)/shard_map/convert_element_type | solution.py:472
Async XLA Ops:
  0.0 77.9 %copy-start = (bf16[16,3712]{1,0:T(8,128)(2,1)S(1)}, bf16[16,3712]{1,0:T(8,128)(2,1)}, u32[]{:S(2)}) copy-start(bf16[16,3712]{1,0:T(8,128)(2,1)} %param.10) | copy-start | bytes 356356

commit v4 on v3

--- a/solution.py
+++ b/solution.py
@@ -45,9 +45,15 @@
     return jnp.where(mask, 1.0, 0.0).astype(jnp.bfloat16)
 
 
+OFFSETS = sorted(
+    ((dy, dz, dx) for dy in range(4) for dz in range(4) for dx in range(2) if dy + dz + dx > 0),
+    key=lambda d: -(min(d[0], 4 - d[0]) + min(d[1], 4 - d[1]) + d[2]),
+)
+
+
 def layer_kernel(chunks, lag, len_ref, x_hbm, wq_hbm, wkv_hbm, wu_hbm, kv_hbm, wd_hbm, wo_hbm, out_ref,
                  xv, wq, wkv, wu, kv, qpart, qr1, qs, qr2, qa, qrecv, us, ur, xs, ux, own, act, perm, iperm, ss, wv, att, asend,
-                 hrecv, heads4, wd, part, r1, s1, part2, r2, s2, part3, own3, r3, wsem, fsend, frecv, asem, brecv, ssem, rsem):
+                 hrecv, heads4, wd, early, part, r1, s1, part2, r2, s2, part3, own3, r3, wsem, fsend, frecv, asem, brecv, ssem, rsem):
     bf = jnp.bfloat16
     gx = lax.axis_index("gx")
     gy = lax.axis_index("gy")
@@ -71,7 +77,7 @@
     for i in range(4):
         loads.append(pltpu.make_async_copy(wu_hbm.at[:, quarter(order[i])], wu.at[i], wsem.at[3 + i]))
     loads.append(pltpu.make_async_copy(kv_hbm, kv, wsem.at[7]))
-    for ld in loads:
+    for ld in loads[:3]:
         ld.start()
     late = []
     for k, (_, lo, w) in enumerate(chunks):
@@ -87,11 +93,9 @@
     pl.semaphore_signal(barrier, inc=1, device_id=core, device_id_type=MESH)
     pl.semaphore_signal(barrier, inc=1, device_id=far, device_id_type=MESH)
 
-    def greet(i, carry):
-        pl.semaphore_signal(barrier, inc=1, device_id=(gx, (gy + i) % 32), device_id_type=MESH)
-        return carry
-
-    lax.fori_loop(1, 32, greet, 0)
+    for dy, dz, dx in OFFSETS:
+        peer = (((y + dy) % 4) * 4 + (z + dz) % 4) * 2 + (xl + dx) % 2
+        pl.semaphore_signal(barrier, inc=1, device_id=(gx, peer), device_id_type=MESH)
 
     moved = {}
 
@@ -104,6 +108,8 @@
 
     for ld in loads[:3]:
         ld.wait()
+    for ld in loads[3:]:
+        ld.start()
     qt = tdot(wq[...], xv[...])
     kvt = tdot(wkv[...], xv[...])
     for o in range(4):
@@ -125,10 +131,6 @@
     up = cdot(xv[...], wu[1])
     moved[2].wait_recv()
     xs[...] = (up + f32(ur[0])).astype(bf)
-    for h in range(4):
-        rows = slice(h * 128, h * 128 + 128)
-        move(4 + h, xs.at[rows], ux.at[rows], far)
-
     for a, b in late:
         a.start()
         b.start()
@@ -148,8 +150,10 @@
     qa[...] = qrows.astype(bf).reshape(32, 16, 128)
     qrecv[gy] = qa[gy]
 
-    def hop_copy(which, src, dst, i, slot):
-        peer = (gy + i) % 32
+    def hop_copy(which, src, dst, i, sending):
+        dy, dz, dx = OFFSETS[i]
+        peer = (((y + dy) % 4) * 4 + (z + dz) % 4) * 2 + (xl + dx) % 2
+        slot = gy if sending else (((y + 4 - dy) % 4) * 4 + (z + 4 - dz) % 4) * 2 + (xl + dx) % 2
         return pltpu.make_async_remote_copy(
             src_ref=src.at[peer],
             dst_ref=dst.at[slot],
@@ -160,27 +164,22 @@
         )
 
     def hop(which, src, dst):
-        def body(i, carry):
-            hop_copy(which, src, dst, i, gy).start()
-            return carry
-
-        lax.fori_loop(1, 32, body, 0)
+        for i in range(31):
+            hop_copy(which, src, dst, i, True).start()
 
     def hop_recv(which, src, dst):
-        def body(i, carry):
-            hop_copy(which, src, dst, i, (gy + 32 - i) % 32).wait_recv()
-            return carry
-
-        lax.fori_loop(1, 32, body, 0)
+        for i in range(30, -1, -1):
+            hop_copy(which, src, dst, i, False).wait_recv()
 
     def hop_sent(which, src, dst):
-        def body(i, carry):
-            hop_copy(which, src, dst, i, gy).wait_send()
-            return carry
-
-        lax.fori_loop(1, 32, body, 0)
+        for i in range(31):
+            hop_copy(which, src, dst, i, True).wait_send()
 
     hop(0, qa, qrecv)
+    for h in range(4):
+        rows = slice(h * 128, h * 128 + 128)
+        move(4 + h, xs.at[rows], ux.at[rows], far)
+
 
     loads[6].wait()
     own[...] = cdot(xv[...], wu[3])
@@ -266,11 +265,20 @@
     move(22, heads4.at[gx], heads4.at[gx], core)
     pass_on(2)
     pass_on(3)
+    for i in range(13, 21):
+        moved[i].wait_recv()
+
+    def ahead(k):
+        _, lo, w = chunks[k]
+        for ld in late[k]:
+            ld.wait()
+        early[k, :, 0:w] = cdot(act[:, 0:1024], wd[0:1024, lo : lo + w])
+
+    ahead(0)
     moved[21].wait_recv()
     move(23, heads4.at[g], heads4.at[g], core)
+    ahead(1)
     moved[22].wait_recv()
-    for i in range(13, 21):
-        moved[i].wait_recv()
     moved[23].wait_recv()
     for h in range(2):
         act[h * 256 : h * 256 + 256, 1024:1280] = jnp.concatenate(
@@ -301,9 +309,12 @@
         cols = pl.ds(lo, w)
         p = coord[s]
         plus, minus = ring[s]
-        for ld in late[k]:
-            ld.wait()
-        acc = cdot(act[...], wd[:, cols])
+        if k < 2:
+            acc = early[k, :, 0:w] + cdot(act[:, 1024:1280], wd[1024:1280, cols])
+        else:
+            for ld in late[k]:
+                ld.wait()
+            acc = cdot(act[...], wd[:, cols])
         acc = acc.astype(jnp.bfloat16)
         for i in range(4):
             for j in range(4):
@@ -398,7 +409,7 @@
     hop_sent(1, asend, hrecv)
 
 
-def layer(normed, w_query, w_keyval, w_out, w_up, w_down, kv_cache, lengths, lanes=512, lag=(0, 2, 4, 6, 8, 10)):
+def layer(normed, w_query, w_keyval, w_out, w_up, w_down, kv_cache, lengths, lanes=1024, lag=(0, 2, 4, 6, 8, 10)):
     width = normed.shape[1]
     bf, f4 = jnp.bfloat16, jnp.float32
     V = pltpu.VMEM
@@ -441,6 +452,7 @@
             V((32, 16, 128), bf),
             V((4, 256, 128), bf),
             V((1280, width), bf),
+            V((2, 512, lanes), f4),
             V((4, 4, 32, width), bf),
             V((6, 2, 32, width), bf),
             V((2, 2, 32, width), bf),

time: 79.7 us -> 76.5 us (0.960)
  Pallas kernels: 77.9 us -> 74.8 us
    pallas_call x1, Pallas kernels: 77.9 us -> 74.8 us  [layer(): pl.pallas_call(functools.partial(layer_kernel, chunks, lag), out_shape=ja...]
where the time goes in v4:
time: 76.5 us; the launch traced here: 76.4 us
  Pallas kernels  74.8 us (98%)
  other arithmetic  1.61 us (2%)
    pallas_call x1, Pallas kernels, layer(): pl.pallas_call(functools.partial(layer_kernel, chunks, lag), out_shape=ja...  74.8 us
    convert_element_type x1, other arithmetic, on_device(): return (residual.astype(jnp.float32) + summed).astype(jnp.bfloat16)  1.61 us

profile of v4, /device:TPU:0, one launch (start us, length us, event | category | flops | bytes accessed | tf_op | source)
XLA Modules:
  0.0 76.4 jit_solution(16625048454447205144)
XLA Ops:
  0.0 0.0 copy-start
  0.0 74.8 %shard_map.91 = f32[16,3712]{1,0:T(8,128)} custom-call(s32[16]{0:T(128)} %len_ref.1, bf16[512,3712]{1,0:T(8,128)(2,1)} %x_hbm.1, bf16[256,3712]{1,0:T(8,128)(2,1)} %bitcast.9, bf16[32,3712]{1,0:T(8,128)(2,1)} %bitcast.11, bf16[3712,1024]{1,0:T(8,128)(2,1)} %wu_hbm.1, bf16[16,2,256,128]{3,2,1,0:T(8,128)(2,1)} %bitcast.8, bf16[1024,3712]{1,0:T(8,128)(2,1)} %wd_hbm.1, ...), custom_call_target="tpu_custom_call" | custom-call | flops 9852420096 | bytes 23756800 | tf_op jit(solution)/shard_map/pallas_call | solution.py:423
  74.8 0.0 copy-done
  74.8 1.6 %add_convert_fusion = bf16[16,3712]{1,0:T(8,128)(2,1)} fusion(f32[16,3712]{1,0:T(8,128)} %shard_map.91, bf16[16,3712]{1,0:T(8,128)(2,1)S(1)} %copy-done), kind=kLoop, calls=%fused_computation | loop fusion | flops 178176 | bytes 475136 | tf_op jit(solution)/shard_map/convert_element_type | solution.py:484
Async XLA Ops:
  0.0 74.8 %copy-start = (bf16[16,3712]{1,0:T(8,128)(2,1)S(1)}, bf16[16,3712]{1,0:T(8,128)(2,1)}, u32[]{:S(2)}) copy-start(bf16[16,3712]{1,0:T(8,128)(2,1)} %param.10) | copy-start | bytes 356356

commit v5 on v4

--- a/solution.py
+++ b/solution.py
@@ -51,9 +51,12 @@
 )
 
 
+PLANE = ((2, 1), (2, 0), (1, 1), (3, 1), (1, 0), (3, 0), (0, 1))
+
+
 def layer_kernel(chunks, lag, len_ref, x_hbm, wq_hbm, wkv_hbm, wu_hbm, kv_hbm, wd_hbm, wo_hbm, out_ref,
                  xv, wq, wkv, wu, kv, qpart, qr1, qs, qr2, qa, qrecv, us, ur, xs, ux, own, act, perm, iperm, ss, wv, att, asend,
-                 hrecv, heads4, wd, early, part, r1, s1, part2, r2, s2, part3, own3, r3, wsem, fsend, frecv, asem, brecv, ssem, rsem):
+                 hrecv, heads4, wd, early, part, r1, s1, part2, r2, wsem, fsend, frecv, asem, brecv, ssem, rsem):
     bf = jnp.bfloat16
     gx = lax.axis_index("gx")
     gy = lax.axis_index("gy")
@@ -292,7 +295,6 @@
         (at((y + 1) % 4, z, xl), at((y + 3) % 4, z, xl)),
         (at(y, (z + 1) % 4, xl), at(y, (z + 3) % 4, xl)),
     )
-    pair = at(y, z, 1 - xl)
     coord = (y, z)
 
     copies = {}
@@ -346,70 +348,48 @@
         s, lo, w = chunks[k]
         cols = pl.ds(lo, w)
         p, q = coord[s], coord[1 - s]
-        plus, minus = ring[1 - s]
         copies[k, 2].wait_recv()
         copies[k, 3].wait_recv()
         copies[k, 4].wait_recv()
         a = f32(part[p, 0:2, :, cols]) + f32(r1[4, :, :, cols]) + f32(r1[3, :, :, cols])
-        part2[0:2, :, cols] = a.astype(jnp.bfloat16)
+        part2[0:2, :, :, cols] = a.astype(bf).reshape(2, 2, 16, w)
         copies[k, 5].wait_recv()
         b = f32(part[p, 2:4, :, cols]) + f32(r1[5, :, :, cols]) + f32(r1[2, :, :, cols])
-        part2[2:4, :, cols] = b.astype(jnp.bfloat16)
-        far, nxt, prv = (q + 2) % 4, (q + 1) % 4, (q + 3) % 4
-        send(k, 6, part2.at[far, 0:16, cols], r2.at[0, :, cols], plus)
-        send(k, 7, part2.at[far, 16:32, cols], r2.at[1, :, cols], minus)
-        send(k, 8, part2.at[nxt, 16:32, cols], r2.at[2, :, cols], plus)
-        send(k, 9, part2.at[prv, 0:16, cols], r2.at[3, :, cols], minus)
-
-    def step_relay2(k):
+        part2[2:4, :, :, cols] = b.astype(bf).reshape(2, 2, 16, w)
+        for i, (dq, dx) in enumerate(PLANE):
+            there, other = (q + dq) % 4, (xl + dx) % 2
+            dev = at(y, there, other) if s == 0 else at(there, z, other)
+            send(k, 6 + i, part2.at[there, other, :, cols], r2.at[i, :, cols], dev)
+
+    def step_last(k):
         s, lo, w = chunks[k]
         cols = pl.ds(lo, w)
         q = coord[1 - s]
-        plus, minus = ring[1 - s]
-        nxt, prv = (q + 1) % 4, (q + 3) % 4
-        copies[k, 6].wait_recv()
-        s2[0, :, cols] = (f32(r2[0, :, cols]) + f32(part2[nxt, 0:16, cols])).astype(jnp.bfloat16)
-        send(k, 10, s2.at[0, :, cols], r2.at[4, :, cols], plus)
-        copies[k, 7].wait_recv()
-        s2[1, :, cols] = (f32(r2[1, :, cols]) + f32(part2[prv, 16:32, cols])).astype(jnp.bfloat16)
-        send(k, 11, s2.at[1, :, cols], r2.at[5, :, cols], minus)
-
-    def step_pair(k):
-        s, lo, w = chunks[k]
-        cols = pl.ds(lo, w)
-        q = coord[1 - s]
-        for i in (8, 9, 10, 11):
-            copies[k, i].wait_recv()
-        a = f32(part2[q, 0:16, cols]) + f32(r2[4, :, cols]) + f32(r2[3, :, cols])
-        b = f32(part2[q, 16:32, cols]) + f32(r2[5, :, cols]) + f32(r2[2, :, cols])
-        part3[0, :, cols] = a.astype(jnp.bfloat16)
-        part3[1, :, cols] = b.astype(jnp.bfloat16)
-        own3[0, :, cols] = a
-        own3[1, :, cols] = b
-        send(k, 12, part3.at[1 - xl, :, cols], r3.at[:, cols], pair)
-
-    def step_last(k):
-        s, lo, w = chunks[k]
-        cols = pl.ds(lo, w)
-        copies[k, 12].wait_recv()
-        out_ref[:, cols] = own3[xl, :, cols] + f32(r3[:, cols])
-
-    steps = (step_compute, step_relay1, step_second, step_relay2, step_pair, step_last)
+        total = f32(part2[q, xl, :, cols])
+        for i in range(6, -1, -1):
+            copies[k, 6 + i].wait_recv()
+            total += f32(r2[i, :, cols])
+        out_ref[:, cols] = total
+
+    steps = (step_compute, step_relay1, step_second, step_last)
     n = len(chunks)
-    for t in range(n + lag[-1]):
+    ends = n + lag[-1]
+    for t in range(ends):
+        if t == n:
+            for i in range(24):
+                moved[i].wait_send()
+            hop_sent(0, qa, qrecv)
+            hop_sent(1, asend, hrecv)
+        if t == ends - 1:
+            for k in range(n):
+                for i in range(13):
+                    copies[k, i].wait_send()
         for fn, d in zip(steps, lag):
             if 0 <= t - d < n:
                 fn(t - d)
-    for k in range(n):
-        for i in range(13):
-            copies[k, i].wait_send()
-    for i in range(24):
-        moved[i].wait_send()
-    hop_sent(0, qa, qrecv)
-    hop_sent(1, asend, hrecv)
-
-
-def layer(normed, w_query, w_keyval, w_out, w_up, w_down, kv_cache, lengths, lanes=1024, lag=(0, 2, 4, 6, 8, 10)):
+
+
+def layer(normed, w_query, w_keyval, w_out, w_up, w_down, kv_cache, lengths, lanes=1024, lag=(0, 2, 4, 6)):
     width = normed.shape[1]
     bf, f4 = jnp.bfloat16, jnp.float32
     V = pltpu.VMEM
@@ -456,12 +436,8 @@
             V((4, 4, 32, width), bf),
             V((6, 2, 32, width), bf),
             V((2, 2, 32, width), bf),
-            V((4, 32, width), bf),
-            V((6, 16, width), bf),
-            V((2, 16, width), bf),
-            V((2, 16, width), bf),
-            V((2, 16, width), f4),
-            V((16, width), bf),
+            V((4, 2, 16, width), bf),
+            V((7, 16, width), bf),
             pltpu.SemaphoreType.DMA((8 + 2 * n,)),
             pltpu.SemaphoreType.DMA((24,)),
             pltpu.SemaphoreType.DMA((24,)),

time: 76.5 us -> 72.9 us (0.953)
  Pallas kernels: 74.8 us -> 71.1 us
    pallas_call x1, Pallas kernels: 74.8 us -> 71.1 us  [layer(): pl.pallas_call(functools.partial(layer_kernel, chunks, lag), out_shape=ja...]
where the time goes in v5:
time: 72.9 us; the launch traced here: 72.7 us
  Pallas kernels  71.1 us (98%)
  other arithmetic  1.61 us (2%)
    pallas_call x1, Pallas kernels, layer(): pl.pallas_call(functools.partial(layer_kernel, chunks, lag), out_shape=ja...  71.1 us
    convert_element_type x1, other arithmetic, on_device(): return (residual.astype(jnp.float32) + summed).astype(jnp.bfloat16)  1.61 us

profile of v5, /device:TPU:0, one launch (start us, length us, event | category | flops | bytes accessed | tf_op | source)
XLA Modules:
  0.0 72.7 jit_solution(5074816713854135727)
XLA Ops:
  0.0 0.0 copy-start
  0.0 71.1 %shard_map.91 = f32[16,3712]{1,0:T(8,128)} custom-call(s32[16]{0:T(128)} %len_ref.1, bf16[512,3712]{1,0:T(8,128)(2,1)} %x_hbm.1, bf16[256,3712]{1,0:T(8,128)(2,1)} %bitcast.9, bf16[32,3712]{1,0:T(8,128)(2,1)} %bitcast.11, bf16[3712,1024]{1,0:T(8,128)(2,1)} %wu_hbm.1, bf16[16,2,256,128]{3,2,1,0:T(8,128)(2,1)} %bitcast.8, bf16[1024,3712]{1,0:T(8,128)(2,1)} %wd_hbm.1, ...), custom_call_target="tpu_custom_call" | custom-call | flops 9852420096 | bytes 23756800 | tf_op jit(solution)/shard_map/pallas_call | solution.py:403
  71.1 0.0 copy-done
  71.1 1.6 %add_convert_fusion = bf16[16,3712]{1,0:T(8,128)(2,1)} fusion(f32[16,3712]{1,0:T(8,128)} %shard_map.91, bf16[16,3712]{1,0:T(8,128)(2,1)S(1)} %copy-done), kind=kLoop, calls=%fused_computation | loop fusion | flops 178176 | bytes 475136 | tf_op jit(solution)/shard_map/convert_element_type | solution.py:460
Async XLA Ops:
  0.0 71.1 %copy-start = (bf16[16,3712]{1,0:T(8,128)(2,1)S(1)}, bf16[16,3712]{1,0:T(8,128)(2,1)}, u32[]{:S(2)}) copy-start(bf16[16,3712]{1,0:T(8,128)(2,1)} %param.10) | copy-start | bytes 356356
